TPU v7x, 128 devices: a whole 4x4x4 slice. The times are simulated.
128 devices in a mesh: dp: 4 (over z), tensor: 32 (over y, x, core).
Axes of the slice: x: 4, y: 4, z: 4, core: 2. Of those that a mesh axis runs over, the one named last changes fastest.
Arguments:
- activations: bfloat16 [8192, 8192], P('dp', 'tensor'), may hold values from -6 to 6
- out_grads: bfloat16 [8192, 28672], P('dp', 'tensor'), may hold values from -6 to 6
- query_inputs: bfloat16 [8192, 2048], P('tensor', 'dp'), may hold values from -0.125 to 0.125
- query_outputs: bfloat16 [28672, 2048], P('tensor', 'dp'), may hold values from -0.0625 to 0.0625
Outputs:
- scores: float32 [8192, 64], P('dp', 'tensor')
All inputs are finite; a program needn't handle non-finite values.
Results may differ from a plain program's by a relative error of at most 0.0003.
Values may be sent and summed in bfloat16 or wider, within the bound.
A program may use at most 192 MiB of HBM per device.

v0:
```python
import math

import jax
import jax.numpy as jnp
from jax import lax
from jax.sharding import PartitionSpec as P

R = 32


def pair_scores(left, right):
    return (left * right).reshape(left.shape[:-1] + (-1, R)).sum(axis=-1) * (1.0 / math.sqrt(R))


def shards(activations, out_grads, query_inputs, query_outputs):
    in_full, out_full = (
        lax.all_gather(query_inputs, "dp", axis=1, tiled=True),
        lax.all_gather(query_outputs, "dp", axis=1, tiled=True),
    )
    part_left = jnp.dot(activations, in_full, preferred_element_type=jnp.float32)
    part_right = jnp.dot(out_grads, out_full, preferred_element_type=jnp.float32)
    left, right = (
        lax.psum_scatter(part_left, "tensor", scatter_dimension=1, tiled=True),
        lax.psum_scatter(part_right, "tensor", scatter_dimension=1, tiled=True),
    )
    scores = pair_scores(left, right)
    return scores


def solution(mesh):
    return jax.shard_map(
        shards,
        mesh=mesh,
        in_specs=(P("dp", "tensor"), P("dp", "tensor"), P("tensor", "dp"), P("tensor", "dp")),
        out_specs=P("dp", "tensor"),
        check_vma=False,
    )
```

profile of v0, /device:TPU:1, one launch (start us, length us, event | category | flops | bytes accessed | tf_op | source)
XLA Modules:
  0.0 327.2 jit_solution(12763021579975626835)
XLA Ops:
  6.5 0.0 copy-start
  6.5 0.0 all-gather.3.cloned.1.call-start
  6.5 0.7 all-gather.3.cloned.1.call-update
  7.3 0.0 all-gather.5.cloned.1.call-start
  7.3 0.7 all-gather.5.cloned.1.call-update
  8.0 0.0 reduce-scatter.3.cloned.1.call-start
  8.1 27.5 %all-gather.3.cloned.1.call-done = bf16[256,2048]{1,0:T(8,128)(2,1)} async-done(((bf16[256,512]{1,0:T(8,128)(2,1)}), bf16[256,2048]{1,0:T(8,128)(2,1)}) %all-gather.3.cloned.1.call-update) | async-done | bytes 1048592 | tf_op jit(solution)/shard_map/all_gather | solution.py:17
  35.6 0.0 copy-done
  35.6 9.3 %fusion = f32[2048,2048]{0,1:T(8,128)} fusion(bf16[2048,256]{1,0:T(8,128)(2,1)S(1)} %copy-done, bf16[256,2048]{1,0:T(8,128)(2,1)} %all-gather.3.cloned.1.call-done), kind=kOutput, calls=%fused_computation.2 | convolution fusion | flops 2147483648 | bytes 18874368 | tf_op jit(solution)/shard_map/dot_general | solution.py:20
  44.9 0.0 reduce-scatter.3.cloned.1.call-update
  44.9 0.0 reduce-scatter.5.cloned.1.call-start
  45.0 37.7 %all-gather.5.cloned.1.call-done = bf16[896,2048]{1,0:T(8,128)(2,1)} async-done(((bf16[896,512]{1,0:T(8,128)(2,1)}), bf16[896,2048]{1,0:T(8,128)(2,1)}) %all-gather.5.cloned.1.call-update) | async-done | bytes 3670032 | tf_op jit(solution)/shard_map/all_gather | solution.py:18
  82.6 15.2 %fusion.1 = f32[2048,2048]{0,1:T(8,128)} fusion(bf16[2048,896]{1,0:T(8,128)(2,1)} %param.5, bf16[896,2048]{1,0:T(8,128)(2,1)} %all-gather.5.cloned.1.call-done), kind=kOutput, calls=%fused_computation.3 | convolution fusion | flops 7516192768 | bytes 24117248 | tf_op jit(solution)/shard_map/dot_general | solution.py:21
  97.8 0.0 reduce-scatter.5.cloned.1.call-update
  97.8 102.6 %reduce-scatter.3.cloned.1.call-done = f32[2048,64]{0,1:T(8,128)} async-done(((f32[2048,2048]{0,1:T(8,128)}), f32[2048,64]{0,1:T(8,128)}) %reduce-scatter.3.cloned.1.call-update) | async-done | bytes 524304 | tf_op jit(solution)/shard_map/reduce_scatter | solution.py:23
  200.4 118.3 %reduce-scatter.5.cloned.1.call-done = f32[2048,64]{0,1:T(8,128)} async-done(((f32[2048,2048]{0,1:T(8,128)}), f32[2048,64]{0,1:T(8,128)}) %reduce-scatter.5.cloned.1.call-update) | async-done | bytes 524304 | tf_op jit(solution)/shard_map/reduce_scatter | solution.py:24
  318.8 1.3 bitcast_reduce_fusion
  320.1 0.6 broadcast_multiply_fusion
Async XLA Ops:
  6.5 29.0 %copy-start = (bf16[2048,256]{1,0:T(8,128)(2,1)S(1)}, bf16[2048,256]{1,0:T(8,128)(2,1)}, u32[]{:S(2)}) copy-start(bf16[2048,256]{1,0:T(8,128)(2,1)} %param.4) | copy-start | bytes 3145732
  6.5 29.0 %all-gather.3.cloned.1.call-start = ((), (), s32[]{:S(2)}) async-start(), calls=%async_computation.2 | async-start | bytes 1310720 | tf_op jit(solution)/shard_map/all_gather | solution.py:17
  7.3 75.4 %all-gather.5.cloned.1.call-start = ((), (), s32[]{:S(2)}) async-start(), calls=%async_computation.4 | async-start | bytes 4587520 | tf_op jit(solution)/shard_map/all_gather | solution.py:18
  8.0 192.4 %reduce-scatter.3.cloned.1.call-start = ((), (), s32[]{:S(2)}) async-start(), calls=%async_computation.3 | async-start | bytes 17301504 | tf_op jit(solution)/shard_map/reduce_scatter | solution.py:23
  44.9 273.9 %reduce-scatter.5.cloned.1.call-start = ((), (), s32[]{:S(2)}) async-start(), calls=%async_computation.5 | async-start | bytes 17301504 | tf_op jit(solution)/shard_map/reduce_scatter | solution.py:24
Sparse Core Ops, SparseCore 0:
  9.0 26.4 all-gather.2
  37.2 45.3 all-gather.4
  86.6 113.8 reduce-scatter.2
  204.2 114.5 reduce-scatter.4
where the time goes:
time: 328 us; the launch traced here: 327 us
  waiting for transfers between devices  288 us (88%)
  matrix products  24.5 us (7%)
  between operations  13.1 us (4%)
    reduce_scatter x1, waiting for transfers between devices, shards(): lax.psum_scatter(part_right, 'tensor', scatter_dimension=1, tiled=True)  118 us
    reduce_scatter x1, waiting for transfers between devices, shards(): lax.psum_scatter(part_left, 'tensor', scatter_dimension=1, tiled=True)  103 us
    all_gather x1, waiting for transfers between devices, shards(): lax.all_gather(query_outputs, 'dp', axis=1, tiled=True)  37.7 us
    all_gather x1, waiting for transfers between devices, shards(): lax.all_gather(query_inputs, 'dp', axis=1, tiled=True)  27.5 us
    dot_general x1, matrix products, shards(): jnp.dot(out_grads, out_full, preferred_element_type=jnp.float32)  15.2 us
    dot_general x1, matrix products, shards(): jnp.dot(activations, in_full, preferred_element_type=jnp.float32)  9.33 us
  transfers between devices with their start and end apart: 4, of which 4 were waited for; matrix products, arithmetic and copies ran while one was open for 7% of the time, Pallas kernels for 0%

commit v1 on v0

v1 whole, which is shorter than its diff:
```python
import functools
import math

import jax
import jax.numpy as jnp
from jax import lax
from jax.experimental import pallas as pl
from jax.experimental.pallas import tpu as pltpu
from jax.sharding import PartitionSpec as P

R = 32
MESH = pl.DeviceIdType.MESH
BF16, F32 = jnp.bfloat16, jnp.float32
SPAN, LOW = 250.0, -124.0
ORDER = (2, 1, 3, 0)
STEP_X, STEP_Y, LAST_Y, LAST_X = 0, 24, 48, 54


def encode(value, box):
    rows = value.shape[0]
    size = jnp.abs(value).reshape(rows // 8, 8, 128)
    top = jnp.max(size, axis=0)
    top = jnp.concatenate([top, top], axis=0).astype(BF16)
    inverse = 1.0 / jnp.maximum(top.astype(F32)[:8], 1e-30)
    part = size * inverse[None]
    root = part * lax.rsqrt(part + 1e-30)
    code = jnp.exp2(root * SPAN + LOW).reshape(rows, 128)
    box[pl.ds(0, rows), :] = jnp.where(value < 0, -code, code).astype(BF16)
    box[pl.ds(rows, 16), :] = top


def decode(box):
    rows = box.shape[0] - 16
    code = box[pl.ds(0, rows), :].astype(F32)
    top = box[pl.ds(rows, 16), :].astype(F32)[:8]
    root = jnp.log(jnp.abs(code)) * (1.0 / (SPAN * math.log(2.0))) - LOW / SPAN
    size = ((root * root).reshape(rows // 8, 8, 128) * top[None]).reshape(rows, 128)
    return jnp.where(code < 0, -size, size)


def kernel(
    act, grad, q_in, q_out, out,
    a, q, part, last, sent, got, mine, theirs,
    load_sem, a_send, a_recv, z_send, z_recv, core_send, core_recv, send_sem, recv_sem, end_send, end_recv,
):
    z, t = lax.axis_index("dp"), lax.axis_index("tensor")
    core, x, y = t % 2, (t // 2) % 4, t // 8
    tokens, w_in = act.shape
    w_out = grad.shape[1]
    half, wide = tokens // 2, w_in + w_out
    rows = half // 4

    def at(dx=0, dy=0, dz=0, other=False):
        index = (((y + dy + 4) % 4) * 4 + (x + dx + 4) % 4) * 2 + ((1 - core) if other else core)
        return ((z + dz + 4) % 4, index)

    own, partner_rows = core * half, (1 - core) * half

    loads = [
        pltpu.make_async_copy(act.at[pl.ds(own, half), :], a.at[:, pl.ds(0, w_in)], load_sem.at[0]),
        pltpu.make_async_copy(grad.at[pl.ds(own, half), :], a.at[:, pl.ds(w_in, w_out)], load_sem.at[1]),
    ]
    for j, step in enumerate(ORDER):
        columns = pl.ds(pl.multiple_of(((x + step) % 4) * 128, 128), 128)
        loads.append(pltpu.make_async_copy(q_in.at[:, columns], q.at[j, z, pl.ds(0, w_in), :], load_sem.at[2 + 2 * j]))
        loads.append(pltpu.make_async_copy(q_out.at[:, columns], q.at[j, z, pl.ds(w_in, w_out), :], load_sem.at[3 + 2 * j]))
    for load in loads:
        load.start()

    barrier = pltpu.get_barrier_semaphore()
    for device in (at(dx=1), at(dx=-1), at(dy=1), at(dy=-1), at(dz=1), at(dz=-1), at(other=True)):
        pl.semaphore_signal(barrier, inc=1, device_id=device, device_id_type=MESH)
    pl.semaphore_wait(barrier, 7)

    def copy(src, dst, send, recv, device):
        return pltpu.make_async_remote_copy(
            src_ref=src, dst_ref=dst, send_sem=send, recv_sem=recv, device_id=device, device_id_type=MESH)

    swaps = [
        copy(act.at[pl.ds(partner_rows, half), :], a.at[:, pl.ds(wide, w_in)], a_send.at[0], a_recv.at[0], at(other=True)),
        copy(grad.at[pl.ds(partner_rows, half), :], a.at[:, pl.ds(wide + w_in, w_out)], a_send.at[1], a_recv.at[1], at(other=True)),
    ]

    def z_copy(j, kind):
        piece, low, count, dz = {
            0: (z, 0, wide, 1),
            1: (z, 0, wide, -1),
            2: ((z + 3) % 4, 0, wide // 2, 1),
            3: ((z + 1) % 4, wide // 2, wide // 2, -1),
        }[kind]
        ref = q.at[j, piece, pl.ds(low, count), :]
        return copy(ref, ref, z_send.at[j, kind], z_recv.at[j, kind], at(dz=dz))

    def z_arrival(j, kind):
        piece, low, count, dz = {
            0: ((z + 3) % 4, 0, wide, 1),
            1: ((z + 1) % 4, 0, wide, -1),
            2: ((z + 2) % 4, 0, wide // 2, 1),
            3: ((z + 2) % 4, wide // 2, wide // 2, -1),
        }[kind]
        ref = q.at[j, piece, pl.ds(low, count), :]
        return copy(ref, ref, z_send.at[j, kind], z_recv.at[j, kind], at(dz=dz))

    def core_copy(j, step):
        piece = (z + step) % 4
        return copy(q.at[j, piece, pl.ds(0, wide), :], q.at[j, piece, pl.ds(wide, wide), :],
                    core_send.at[j, step], core_recv.at[j, step], at(other=True))

    for swap in swaps:
        swap.start()
    for j in range(4):
        loads[2 + 2 * j].wait()
        loads[3 + 2 * j].wait()
        z_copy(j, 0).start()
        z_copy(j, 1).start()
        core_copy(j, 0).start()
    loads[0].wait()
    loads[1].wait()

    def pass_near(j):
        z_arrival(j, 0).wait_recv()
        z_copy(j, 2).start()
        core_copy(j, 3).start()
        z_arrival(j, 1).wait_recv()
        z_copy(j, 3).start()
        core_copy(j, 1).start()

    def pass_far(j):
        z_arrival(j, 2).wait_recv()
        z_arrival(j, 3).wait_recv()
        core_copy(j, 2).start()

    def await_core(j):
        for step in (0, 3, 1, 2):
            core_copy(j, step).wait_recv()

    def project(j):
        @pl.loop(0, 4)
        def _(i):
            pair, twin = i // 2, i % 2
            line = pl.ds(pl.multiple_of(pair * 2 * rows, 2 * rows), 2 * rows)

            def product(low, count):
                total = None
                for base in (low, low + wide):
                    left = a[line, pl.ds(base, count)]
                    right = jnp.concatenate([q[j, 2 * twin, pl.ds(base, count), :], q[j, 2 * twin + 1, pl.ds(base, count), :]], axis=1)
                    term = jnp.dot(left, right, preferred_element_type=F32)
                    total = term if total is None else total + term
                return total

            for h, (low, count) in enumerate(((0, w_in), (w_in, w_out))):
                value = product(low, count)
                for g in range(2):
                    for n in range(2):
                        part[j, 2 * pair + g, 2 * twin + n, h] = value[g * rows:(g + 1) * rows, n * 128:(n + 1) * 128]

    def message(m, device):
        return copy(sent.at[m], got.at[m], send_sem.at[m], recv_sem.at[m], device)

    def arrived(m):
        message(m, at(dx=1)).wait_recv()

    def send(m, source, device, add=None):
        if add is not None:
            arrived(add)

        @pl.loop(0, 2)
        def _(h):
            value = source[h]
            if add is not None:
                value = value + decode(got.at[add, h])
            encode(value, sent.at[m, h])

        message(m, device).start()

    def finish(target, source, first, second):
        arrived(first)
        arrived(second)

        @pl.loop(0, 2)
        def _(h):
            target[h] = source[h] + decode(got.at[first, h]) + decode(got.at[second, h])

    def along_y(base, stride, j, source, target):
        up, down = at(dy=1), at(dy=-1)
        far, after, before = (y + 2) % 4, (y + 1) % 4, (y + 3) % 4
        slot = lambda kind: base + kind * stride + j
        send(slot(0), source(0, far), up)
        send(slot(3), source(1, far), down)
        send(slot(2), source(1, after), up)
        send(slot(5), source(0, before), down)
        send(slot(1), source(0, after), up, add=slot(0))
        send(slot(4), source(1, before), down, add=slot(3))
        finish(target(0), source(0, y), slot(1), slot(5))
        finish(target(1), source(1, y), slot(4), slot(2))

    def step_x(kind, g, n, j, add=None):
        device = at(dx=1) if kind < 3 else at(dx=-1)
        send(STEP_X + kind * 4 + n, part.at[j, g, n], device, add=None if add is None else STEP_X + add * 4 + n)

    for swap in swaps:
        swap.wait_recv()
    right, left = at(dx=1), at(dx=-1)
    for j in range(4):
        pass_near(j)
        pass_far(j)
        await_core(j)
        project(j)

        @pl.loop(0, 4)
        def _(n):
            if ORDER[j] == 2:
                step_x(0, 0, n, j)
                step_x(3, 1, n, j)
            elif ORDER[j] == 1:
                step_x(2, 1, n, j)
                step_x(1, 0, n, j, add=0)
            elif ORDER[j] == 3:
                step_x(5, 0, n, j)
                step_x(4, 1, n, j, add=3)
            else:
                finish(part.at[j, 0, n], part.at[j, 0, n], STEP_X + 1 * 4 + n, STEP_X + 5 * 4 + n)
                finish(part.at[j, 1, n], part.at[j, 1, n], STEP_X + 4 * 4 + n, STEP_X + 2 * 4 + n)

        along_y(STEP_Y, 4, j, lambda b, n: part.at[j, 2 + b, n], lambda b: last.at[j, b])
        if ORDER[j] == 2:
            send(LAST_X + 0, last.at[j, 0], right)
            send(LAST_X + 3, last.at[j, 1], left)
        elif ORDER[j] == 1:
            send(LAST_X + 2, last.at[j, 1], right)
            send(LAST_X + 1, last.at[j, 0], right, add=LAST_X + 0)
        elif ORDER[j] == 3:
            send(LAST_X + 5, last.at[j, 0], left)
            send(LAST_X + 4, last.at[j, 1], left, add=LAST_X + 3)
        else:
            finish(last.at[j, 0], last.at[j, 0], LAST_X + 1, LAST_X + 5)
            finish(last.at[j, 1], last.at[j, 1], LAST_X + 4, LAST_X + 2)
            along_y(LAST_Y, 1, 0, lambda b, n: part.at[j, b, n], lambda b: last.at[0, b])

    query = lax.broadcasted_iota(jnp.int32, (8, 128), 0)
    owner = lax.broadcasted_iota(jnp.int32, (8, 128), 1) // R

    def pick(which):
        return jnp.where((owner == query + 2 * which) & (query < 2), 1.0, 0.0).astype(BF16)

    for g in range(4):
        value = last.at[0 if g < 2 else 3, g % 2]
        product = value[0] * value[1] * (1.0 / math.sqrt(R))
        high = product.astype(BF16)
        rest = product - high.astype(F32)
        middle = rest.astype(BF16)
        low = (rest - middle.astype(F32)).astype(BF16)
        for which, target in ((core, mine), (1 - core, theirs)):
            mask = pick(which)
            total = None
            for term in (low, middle, high):
                s = lax.dot_general(mask, term, (((1,), (1,)), ((), ())), preferred_element_type=F32)
                total = s if total is None else total + s
            target[0, :, pl.ds(g * rows, rows)] = total
    final = copy(theirs.at[0], theirs.at[1], end_send, end_recv, at(other=True))
    final.start()
    out[:, pl.ds(pl.multiple_of(own, half), half)] = mine[0]
    final.wait_recv()
    out[:, pl.ds(pl.multiple_of(partner_rows, half), half)] = theirs[1]

    final.wait_send()
    for swap in swaps:
        swap.wait_send()
    for j in range(4):
        for k in range(4):
            z_copy(j, k).wait_send()
            core_copy(j, k).wait_send()

    @pl.loop(0, 60)
    def _(m):
        message(m, right).wait_send()


def scores_of(act, grad, q_in, q_out):
    tokens, w_in = act.shape
    w_out = grad.shape[1]
    half, wide = tokens // 2, w_in + w_out
    rows = half // 4
    dma = pltpu.SemaphoreType.DMA
    scores = pl.pallas_call(
        kernel,
        out_shape=jax.ShapeDtypeStruct((8, tokens), F32),
        in_specs=[pl.BlockSpec(memory_space=pl.ANY)] * 4,
        out_specs=pl.BlockSpec(memory_space=pltpu.VMEM),
        scratch_shapes=[
            pltpu.VMEM((half, 2 * wide), BF16),
            pltpu.VMEM((4, 4, 2 * wide, 128), BF16),
            pltpu.VMEM((4, 4, 4, 2, rows, 128), F32),
            pltpu.VMEM((4, 2, 2, rows, 128), F32),
            pltpu.VMEM((60, 2, rows + 16, 128), BF16),
            pltpu.VMEM((60, 2, rows + 16, 128), BF16),
            pltpu.VMEM((1, 8, half), F32),
            pltpu.VMEM((2, 8, half), F32),
            dma((10,)), dma((2,)), dma((2,)),
            dma((4, 4)), dma((4, 4)), dma((4, 4)), dma((4, 4)),
            dma((60,)), dma((60,)), dma, dma,
        ],
        compiler_params=pltpu.CompilerParams(
            collective_id=0, has_side_effects=True, vmem_limit_bytes=58 * 1024 * 1024),
        cost_estimate=pl.CostEstimate(flops=2 * tokens * wide * 2048, bytes_accessed=6 * 2**20, transcendentals=0),
    )(act, grad, q_in, q_out)
    return scores[:2].T


def solution(mesh):
    return jax.shard_map(
        scores_of,
        mesh=mesh,
        in_specs=(P("dp", "tensor"), P("dp", "tensor"), P("tensor", "dp"), P("tensor", "dp")),
        out_specs=P("dp", "tensor"),
        check_vma=False,
    )
```

time: 328 us -> 147 us (0.45)
  waiting for transfers between devices: 288 us -> 0 us
  Pallas kernels: 0 us -> 145 us
  matrix products: 24.5 us -> 0 us
  between operations: 13.1 us -> 0.01 us
    reduce_scatter x2 -> x0, waiting for transfers between devices: 221 us -> none  [the longest x1 118 us: shards(): lax.psum_scatter(part_right, 'tensor', scatter_dimension=1, tiled=True)]
    pallas_call x0 -> x1, Pallas kernels: none -> 145 us  [scores_of(): pl.pallas_call(kernel, out_shape=jax.ShapeDtypeStruct((8, tokens), F32),...]
    all_gather x2 -> x0, waiting for transfers between devices: 65.2 us -> none  [the longest x1 37.7 us: shards(): lax.all_gather(query_outputs, 'dp', axis=1, tiled=True)]
    dot_general x2 -> x0, matrix products: 24.5 us -> none  [the longest x1 15.2 us: shards(): jnp.dot(out_grads, out_full, preferred_element_type=jnp.float32)]
  transfers between devices with their start and end apart: 4 -> 0, of which waited for: 4 -> 0; matrix products, arithmetic and copies ran while one was open for 7% -> 0% of each run, Pallas kernels for 0% -> 0%
where the time goes in v1:
time: 147 us
  Pallas kernels  145 us (99%)
    pallas_call x1, Pallas kernels, scores_of(): pl.pallas_call(kernel, out_shape=jax.ShapeDtypeStruct((8, tokens), F32),...  145 us

profile of v1, /device:TPU:1, one launch (start us, length us, event | category | flops | bytes accessed | tf_op | source)
XLA Modules:
  0.0 146.7 jit_solution(248698325089952474)
XLA Ops:
  0.0 145.3 %shard_map.46 = f32[8,2048]{1,0:T(8,128)} custom-call(bf16[2048,256]{1,0:T(8,128)(2,1)} %act.1, bf16[2048,896]{1,0:T(8,128)(2,1)} %grad.1, bf16[256,512]{1,0:T(8,128)(2,1)} %q_in.1, bf16[896,512]{1,0:T(8,128)(2,1)} %q_out.1), custom_call_target="tpu_custom_call" | custom-call | flops 9663676416 | bytes 6291456 | tf_op jit(solution)/shard_map/pallas_call | solution.py:286
  145.3 1.4 slice_bitcast_fusion

commit v2 on v1

v2 whole, which is shorter than its diff:
```python
import functools
import math

import jax
import jax.numpy as jnp
from jax import lax
from jax.experimental import pallas as pl
from jax.experimental.pallas import tpu as pltpu
from jax.sharding import PartitionSpec as P

R = 32
MESH = pl.DeviceIdType.MESH
BF16, F32 = jnp.bfloat16, jnp.float32
SPAN, LOW = 250.0, -124.0
ORDER = (2, 1, 3, 0)
ROWS_X = 288
TASKS = (
    ('own', 0), ('own', 1), ('near', 0), ('xr', 2, 0), ('xr', 1, 0), ('xr', 3, 0), ('pn', 0), ('xr', 2, 1),
    ('xr', 2, 3), ('near', 1), ('xa', 1, 0), ('xa', 3, 0), ('pn', 1), ('far', 0), ('xr', 1, 1), ('xr', 1, 3),
    ('pf', 0), ('xr', 2, 2), ('xa', 1, 1), ('yr', 0), ('near', 2), ('xa', 1, 3), ('pn', 2), ('far', 1), ('xr', 3, 3),
    ('xr', 3, 1), ('ya', 1, 0), ('ya', 3, 0), ('xa', 3, 3), ('pf', 1), ('yr', 1), ('xr', 1, 2), ('xa', 3, 1),
    ('xf', 0), ('near', 3), ('yf', 0), ('lx', 0), ('pn', 3), ('far', 2), ('ya', 1, 1), ('ya', 3, 1), ('xa', 1, 2),
    ('pf', 2), ('yr', 2), ('xr', 3, 2), ('xa', 3, 2), ('far', 3), ('yf', 1), ('lx', 2), ('pf', 3), ('yr', 3),
    ('ya', 3, 2), ('xf', 3), ('xf', 1), ('ya', 1, 2), ('lx', 1), ('ya', 1, 3), ('ya', 3, 3), ('xf', 2), ('ly', 0),
    ('yf', 2), ('lx', 4), ('lx', 5), ('yf', 3), ('ly', 1), ('ly', 4), ('lx', 9), ('ly', 9),
)


def encode(value, box):
    rows = value.shape[0]
    size = jnp.abs(value).reshape(rows // 8, 8, 128)
    top = jnp.max(size, axis=0)
    top = jnp.concatenate([top, top], axis=0).astype(BF16)
    inverse = 1.0 / jnp.maximum(top.astype(F32)[:8], 1e-30)
    part = size * inverse[None]
    root = part * lax.rsqrt(part + 1e-30)
    code = jnp.exp2(root * SPAN + LOW).reshape(rows, 128)
    box[pl.ds(0, rows), :] = jnp.where(value < 0, -code, code).astype(BF16)
    box[pl.ds(rows, 16), :] = top


def decode(box):
    rows = box.shape[0] - 16
    code = box[pl.ds(0, rows), :].astype(F32)
    top = box[pl.ds(rows, 16), :].astype(F32)[:8]
    root = jnp.log(jnp.abs(code)) * (1.0 / (SPAN * math.log(2.0))) - LOW / SPAN
    size = ((root * root).reshape(rows // 8, 8, 128) * top[None]).reshape(rows, 128)
    return jnp.where(code < 0, -size, size)


def kernel(
    act, grad, q_in, q_out, out,
    a, q, part, sent_x, got_x, sent_y, got_y, mine, theirs,
    load_sem, a_send, a_recv, z_send, z_recv, core_send, core_recv,
    send_x_sem, recv_x_sem, send_y_sem, recv_y_sem, end_send, end_recv,
):
    box_x, box_y = (sent_x, got_x, send_x_sem, recv_x_sem), (sent_y, got_y, send_y_sem, recv_y_sem)
    z, t = lax.axis_index("dp"), lax.axis_index("tensor")
    core, x, y = t % 2, (t // 2) % 4, t // 8
    tokens, w_in = act.shape
    w_out = grad.shape[1]
    half, wide = tokens // 2, w_in + w_out
    rx, ry = ROWS_X, half // 2 - ROWS_X

    def at(dx=0, dy=0, dz=0, other=False):
        index = (((y + dy + 4) % 4) * 4 + (x + dx + 4) % 4) * 2 + ((1 - core) if other else core)
        return ((z + dz + 4) % 4, index)

    own, partner_rows = core * half, (1 - core) * half

    loads = [
        pltpu.make_async_copy(act.at[pl.ds(own, half), :], a.at[:, pl.ds(0, w_in)], load_sem.at[0]),
        pltpu.make_async_copy(grad.at[pl.ds(own, half), :], a.at[:, pl.ds(w_in, w_out)], load_sem.at[1]),
    ]
    for j, step in enumerate(ORDER):
        columns = pl.ds(pl.multiple_of(((x + step) % 4) * 128, 128), 128)
        loads.append(pltpu.make_async_copy(q_in.at[:, columns], q.at[j, z, pl.ds(0, w_in), :], load_sem.at[2 + 2 * j]))
        loads.append(pltpu.make_async_copy(q_out.at[:, columns], q.at[j, z, pl.ds(w_in, w_out), :], load_sem.at[3 + 2 * j]))
    for load in loads:
        load.start()

    barrier = pltpu.get_barrier_semaphore()
    for device in (at(dx=1), at(dx=-1), at(dy=1), at(dy=-1), at(dz=1), at(dz=-1), at(other=True)):
        pl.semaphore_signal(barrier, inc=1, device_id=device, device_id_type=MESH)
    pl.semaphore_wait(barrier, 7)

    def copy(src, dst, send, recv, device):
        return pltpu.make_async_remote_copy(
            src_ref=src, dst_ref=dst, send_sem=send, recv_sem=recv, device_id=device, device_id_type=MESH)

    swaps = [
        copy(act.at[pl.ds(partner_rows, half), :], a.at[:, pl.ds(wide, w_in)], a_send.at[0], a_recv.at[0], at(other=True)),
        copy(grad.at[pl.ds(partner_rows, half), :], a.at[:, pl.ds(wide + w_in, w_out)], a_send.at[1], a_recv.at[1], at(other=True)),
    ]

    def z_copy(j, kind):
        piece, low, count, dz = {
            0: (z, 0, wide, 1),
            1: (z, 0, wide, -1),
            2: ((z + 3) % 4, 0, wide // 2, 1),
            3: ((z + 1) % 4, wide // 2, wide // 2, -1),
        }[kind]
        ref = q.at[j, piece, pl.ds(low, count), :]
        return copy(ref, ref, z_send.at[j, kind], z_recv.at[j, kind], at(dz=dz))

    def z_arrival(j, kind):
        piece, low, count, dz = {
            0: ((z + 3) % 4, 0, wide, 1),
            1: ((z + 1) % 4, 0, wide, -1),
            2: ((z + 2) % 4, 0, wide // 2, 1),
            3: ((z + 2) % 4, wide // 2, wide // 2, -1),
        }[kind]
        ref = q.at[j, piece, pl.ds(low, count), :]
        return copy(ref, ref, z_send.at[j, kind], z_recv.at[j, kind], at(dz=dz))

    def core_copy(j, step):
        piece = (z + step) % 4
        return copy(q.at[j, piece, pl.ds(0, wide), :], q.at[j, piece, pl.ds(wide, wide), :],
                    core_send.at[j, step], core_recv.at[j, step], at(other=True))

    for j in range(4):
        loads[2 + 2 * j].wait()
        loads[3 + 2 * j].wait()
        if j < 2:
            z_copy(j, 0).start()
            z_copy(j, 1).start()
        core_copy(j, 0).start()
        if j == 1:
            for swap in swaps:
                swap.start()

    def pass_near(j):
        z_arrival(j, 0).wait_recv()
        z_copy(j, 2).start()
        core_copy(j, 3).start()
        z_arrival(j, 1).wait_recv()
        z_copy(j, 3).start()
        core_copy(j, 1).start()
        if j < 2:
            z_copy(j + 2, 0).start()
            z_copy(j + 2, 1).start()

    def pass_far(j):
        z_arrival(j, 2).wait_recv()
        z_arrival(j, 3).wait_recv()
        core_copy(j, 2).start()

    def project(pieces):
        for j, i in pieces:
            core_copy(j, i).wait_recv()
        block = half // 2

        @pl.loop(0, 2)
        def _(i):
            line = pl.ds(pl.multiple_of(i * block, block), block)
            for h, (low, count) in enumerate(((0, w_in), (w_in, w_out))):
                total = None
                for base in (low, low + wide):
                    right = [q[j, (z + step) % 4, pl.ds(base, count), :] for j, step in pieces]
                    right = right[0] if len(right) == 1 else jnp.concatenate(right, axis=1)
                    term = jnp.dot(a[line, pl.ds(base, count)], right, preferred_element_type=F32)
                    total = term if total is None else total + term
                for k, (j, step) in enumerate(pieces):
                    part[j, (z + step) % 4, h, line, :] = total[:, k * 128:(k + 1) * 128]

    def message(box, m, device):
        sent, got, out_sem, in_sem = box
        return copy(sent.at[m], got.at[m], out_sem.at[m], in_sem.at[m], device)

    def arrived(box, m):
        message(box, m, at(dx=1)).wait_recv()

    def send(box, m, source, device, add=None):
        sent, got = box[:2]
        if add is not None:
            arrived(box, add)

        @pl.loop(0, 2)
        def _(h):
            value = source[h]
            if add is not None:
                value = value + decode(got.at[add, h])
            encode(value, sent.at[m, h])

        message(box, m, device).start()

    def finish(box, target, first, second):
        got = box[1]
        arrived(box, first)
        arrived(box, second)

        @pl.loop(0, 2)
        def _(h):
            target[h] = target[h] + decode(got.at[first, h]) + decode(got.at[second, h])

    right, left = at(dx=1), at(dx=-1)
    up, down = at(dy=1), at(dy=-1)

    def x_part(j, n, b):
        return part.at[j, n, :, pl.ds(b * rx, rx), :]

    def y_part(j, n, b):
        return part.at[j, n, :, pl.ds(2 * rx + b * ry, ry), :]

    def send_x(kind, j, n, b, add=None):
        send(box_x, kind * 4 + n, x_part(j, n, b), right if kind < 3 else left, None if add is None else add * 4 + n)

    def send_y(kind, j, n, b, add=None):
        send(box_y, kind * 4 + j, y_part(j, n, b), up if kind < 3 else down, None if add is None else add * 4 + j)

    def last_x(kind, j, b, add=None):
        send(box_y, 24 + kind, y_part(j, y, b), right if kind < 3 else left, None if add is None else 24 + add)

    def last_y(kind, n, b, add=None):
        send(box_x, 24 + kind, x_part(3, n, b), up if kind < 3 else down, None if add is None else 24 + add)

    far, after, before = (y + 2) % 4, (y + 1) % 4, (y + 3) % 4

    def task(name, *index):
        if name == "near":
            pass_near(index[0])
        elif name == "far":
            pass_far(index[0])
        elif name == "own":
            if index[0] == 0:
                for load in loads[:2]:
                    load.wait()
                for swap in swaps:
                    swap.wait_recv()
            pieces = [(2 * index[0], 0), (2 * index[0] + 1, 0)]
            project(pieces)
        elif name == "pn":
            project([(index[0], 3), (index[0], 1)])
        elif name == "pf":
            project([(index[0], 2)])
        elif name == "xr":
            kind, i = index
            n = (z + i) % 4
            if kind == 2:
                send_x(0, 0, n, 0)
                send_x(3, 0, n, 1)
            elif kind == 1:
                send_x(2, 1, n, 1)
            else:
                send_x(5, 2, n, 0)
        elif name == "xa":
            kind, i = index
            n = (z + i) % 4
            if kind == 1:
                send_x(1, 1, n, 0, add=0)
            else:
                send_x(4, 2, n, 1, add=3)
        elif name == "xf":
            n = (z + index[0]) % 4
            finish(box_x, x_part(3, n, 0), 4 + n, 20 + n)
            finish(box_x, x_part(3, n, 1), 16 + n, 8 + n)
        elif name == "yr":
            j = index[0]
            send_y(0, j, far, 0)
            send_y(3, j, far, 1)
            send_y(2, j, after, 1)
            send_y(5, j, before, 0)
        elif name == "ya":
            kind, j = index
            if kind == 1:
                send_y(1, j, after, 0, add=0)
            else:
                send_y(4, j, before, 1, add=3)
        elif name == "yf":
            j = index[0]
            finish(box_y, y_part(j, y, 0), 4 + j, 20 + j)
            finish(box_y, y_part(j, y, 1), 16 + j, 8 + j)
        elif name == "lx":
            kind = index[0]
            if kind == 0:
                last_x(0, 0, 0)
                last_x(3, 0, 1)
            elif kind == 2:
                last_x(2, 1, 1)
            elif kind == 5:
                last_x(5, 2, 0)
            elif kind == 1:
                last_x(1, 1, 0, add=0)
            elif kind == 4:
                last_x(4, 2, 1, add=3)
            else:
                finish(box_y, y_part(3, y, 0), 24 + 1, 24 + 5)
                finish(box_y, y_part(3, y, 1), 24 + 4, 24 + 2)
        else:
            kind = index[0]
            if kind == 0:
                last_y(0, far, 0)
                last_y(3, far, 1)
                last_y(2, after, 1)
                last_y(5, before, 0)
            elif kind == 1:
                last_y(1, after, 0, add=0)
            elif kind == 4:
                last_y(4, before, 1, add=3)
            else:
                finish(box_x, x_part(3, y, 0), 24 + 1, 24 + 5)
                finish(box_x, x_part(3, y, 1), 24 + 4, 24 + 2)

    for name, *index in TASKS:
        task(name, *index)

    query = lax.broadcasted_iota(jnp.int32, (8, 128), 0)
    owner = lax.broadcasted_iota(jnp.int32, (8, 128), 1) // R

    def pick(which):
        return jnp.where((owner == query + 2 * which) & (query < 2), 1.0, 0.0).astype(BF16)

    rows = half // 4
    for g in range(4):
        line = pl.ds(g * rows, rows)
        product = part[3, y, 0, line, :] * part[3, y, 1, line, :] * (1.0 / math.sqrt(R))
        high = product.astype(BF16)
        rest = product - high.astype(F32)
        middle = rest.astype(BF16)
        low = (rest - middle.astype(F32)).astype(BF16)
        for which, target in ((core, mine), (1 - core, theirs)):
            mask = pick(which)
            total = None
            for term in (low, middle, high):
                s = lax.dot_general(mask, term, (((1,), (1,)), ((), ())), preferred_element_type=F32)
                total = s if total is None else total + s
            target[0, :, pl.ds(g * rows, rows)] = total
    final = copy(theirs.at[0], theirs.at[1], end_send, end_recv, at(other=True))
    final.start()
    out[:, pl.ds(pl.multiple_of(own, half), half)] = mine[0]
    final.wait_recv()
    out[:, pl.ds(pl.multiple_of(partner_rows, half), half)] = theirs[1]

    final.wait_send()
    for swap in swaps:
        swap.wait_send()
    for j in range(4):
        for k in range(4):
            z_copy(j, k).wait_send()
            core_copy(j, k).wait_send()

    @pl.loop(0, 30)
    def _(m):
        message(box_x, m, right).wait_send()
        message(box_y, m, right).wait_send()


def scores_of(act, grad, q_in, q_out):
    tokens, w_in = act.shape
    w_out = grad.shape[1]
    half, wide = tokens // 2, w_in + w_out
    rx, ry = ROWS_X, half // 2 - ROWS_X
    dma = pltpu.SemaphoreType.DMA
    scores = pl.pallas_call(
        kernel,
        out_shape=jax.ShapeDtypeStruct((8, tokens), F32),
        in_specs=[pl.BlockSpec(memory_space=pl.ANY)] * 4,
        out_specs=pl.BlockSpec(memory_space=pltpu.VMEM),
        scratch_shapes=[
            pltpu.VMEM((half, 2 * wide), BF16),
            pltpu.VMEM((4, 4, 2 * wide, 128), BF16),
            pltpu.VMEM((4, 4, 2, half, 128), F32),
            pltpu.VMEM((30, 2, rx + 16, 128), BF16),
            pltpu.VMEM((30, 2, rx + 16, 128), BF16),
            pltpu.VMEM((30, 2, ry + 16, 128), BF16),
            pltpu.VMEM((30, 2, ry + 16, 128), BF16),
            pltpu.VMEM((1, 8, half), F32),
            pltpu.VMEM((2, 8, half), F32),
            dma((10,)), dma((2,)), dma((2,)),
            dma((4, 4)), dma((4, 4)), dma((4, 4)), dma((4, 4)),
            dma((30,)), dma((30,)), dma((30,)), dma((30,)), dma, dma,
        ],
        compiler_params=pltpu.CompilerParams(
            collective_id=0, has_side_effects=True, vmem_limit_bytes=58 * 1024 * 1024),
        cost_estimate=pl.CostEstimate(flops=2 * tokens * wide * 2048, bytes_accessed=6 * 2**20, transcendentals=0),
    )(act, grad, q_in, q_out)
    return scores[:2].T


def solution(mesh):
    return jax.shard_map(
        scores_of,
        mesh=mesh,
        in_specs=(P("dp", "tensor"), P("dp", "tensor"), P("tensor", "dp"), P("tensor", "dp")),
        out_specs=P("dp", "tensor"),
        check_vma=False,
    )
```

time: 147 us -> 83.7 us (0.57)
  Pallas kernels: 145 us -> 82.1 us
    pallas_call x1, Pallas kernels: 145 us -> 82.1 us  [scores_of(): pl.pallas_call(kernel, out_shape=jax.ShapeDtypeStruct((8, tokens), F32),...]
where the time goes in v2:
time: 83.7 us; the launch traced here: 83.6 us
  Pallas kernels  82.1 us (98%)
  local copies, waits for them, and re-layouts  1.45 us (2%)
    pallas_call x1, Pallas kernels, scores_of(): pl.pallas_call(kernel, out_shape=jax.ShapeDtypeStruct((8, tokens), F32),...  82.1 us

profile of v2, /device:TPU:1, one launch (start us, length us, event | category | flops | bytes accessed | tf_op | source)
XLA Modules:
  0.0 83.6 jit_solution(5722697054081588638)
XLA Ops:
  0.0 82.1 %shard_map.46 = f32[8,2048]{1,0:T(8,128)} custom-call(bf16[2048,256]{1,0:T(8,128)(2,1)} %act.1, bf16[2048,896]{1,0:T(8,128)(2,1)} %grad.1, bf16[256,512]{1,0:T(8,128)(2,1)} %q_in.1, bf16[896,512]{1,0:T(8,128)(2,1)} %q_out.1), custom_call_target="tpu_custom_call" | custom-call | flops 9663676416 | bytes 6291456 | tf_op jit(solution)/shard_map/pallas_call | solution.py:354
  82.1 1.4 %slice_bitcast_fusion = f32[2048,2]{0,1:T(2,128)} fusion(f32[8,2048]{1,0:T(8,128)} %shard_map.46), kind=kLoop, calls=%fused_computation | loop fusion | bytes 32768 | tf_op jit(solution)/shard_map/transpose | solution.py:377

commit v3 on v2

v3 whole, which is shorter than its diff:
```python
import functools
import math

import jax
import jax.numpy as jnp
from jax import lax
from jax.experimental import pallas as pl
from jax.experimental.pallas import tpu as pltpu
from jax.sharding import PartitionSpec as P

R = 32
MESH = pl.DeviceIdType.MESH
BF16, F32 = jnp.bfloat16, jnp.float32
SPAN, LOW = 250.0, -124.0
ORDER = (2, 1, 3, 0)
ROWS_X = 288
TASKS = (
    ('own', 0), ('xr', 1, 0), ('xr', 2, 0), ('own', 1), ('xr', 3, 0), ('own', 2), ('y', 0, 0, 0), ('own', 3),
    ('near', 0), ('y', 0, 1, 0), ('y', 0, 2, 0), ('y', 0, 3, 0), ('pn', 0), ('xr', 2, 3), ('xa', 3, 0),
    ('y', 0, 0, 3), ('xr', 2, 1), ('y', 1, 0, 0), ('y', 0, 0, 1), ('xa', 1, 0), ('near', 1), ('y', 1, 1, 0),
    ('pn', 1), ('xr', 1, 3), ('xa', 1, 3), ('y', 0, 1, 3), ('xr', 1, 1), ('y', 0, 1, 1), ('far', 0), ('y', 1, 3, 0),
    ('y', 1, 2, 0), ('xa', 1, 1), ('pf', 0), ('y', 0, 0, 2), ('y', 1, 0, 3), ('xr', 2, 2), ('xf', 0), ('ly', 0, 0),
    ('near', 2), ('y', 1, 0, 1), ('y', 2, 0, 0), ('pn', 2), ('far', 1), ('y', 0, 2, 1), ('xa', 3, 3), ('y', 0, 2, 3),
    ('xa', 3, 1), ('y', 2, 0, 3), ('pf', 1), ('y', 0, 1, 2), ('y', 1, 1, 1), ('xr', 1, 2), ('xr', 3, 1),
    ('y', 1, 1, 3), ('ly', 1, 0), ('xr', 3, 3), ('y', 2, 3, 0), ('y', 1, 0, 2), ('y', 2, 0, 1), ('y', 2, 1, 0),
    ('near', 3), ('y', 2, 2, 0), ('y', 1, 1, 2), ('pn', 3), ('far', 2), ('y', 0, 3, 1), ('y', 0, 3, 3),
    ('y', 2, 1, 3), ('y', 2, 1, 1), ('pf', 2), ('y', 0, 2, 2), ('xr', 3, 2), ('y', 1, 2, 1), ('y', 2, 0, 2),
    ('xa', 1, 2), ('far', 3), ('y', 1, 2, 3), ('xa', 3, 2), ('lx', 0), ('xf', 1), ('pf', 3), ('y', 0, 3, 2),
    ('ly', 0, 1), ('xf', 3), ('ly', 0, 3), ('y', 1, 2, 2), ('y', 2, 1, 2), ('lx', 2), ('ly', 2, 0), ('y', 1, 3, 3),
    ('y', 1, 3, 1), ('y', 2, 2, 1), ('y', 2, 2, 3), ('y', 1, 3, 2), ('lx', 1), ('xf', 2), ('ly', 0, 2), ('ly', 1, 1),
    ('ly', 1, 3), ('y', 2, 2, 2), ('lx', 5), ('lx', 4), ('y', 2, 3, 2), ('y', 2, 3, 3), ('y', 2, 3, 1), ('ly', 1, 2),
    ('ly', 2, 3), ('ly', 2, 1), ('lx', 9), ('ly', 2, 2),
)


def encode(value, box, top_box):
    rows = value.shape[0]
    size = jnp.abs(value).reshape(rows // 8, 8, 128)
    top = jnp.max(size, axis=0).astype(BF16).astype(F32)
    top_box[...] = top
    part = size * (1.0 / jnp.maximum(top, 1e-30))[None]
    root = part * lax.rsqrt(part + 1e-30)
    code = jnp.exp2(root * SPAN + LOW).reshape(rows, 128)
    box[...] = jnp.where(value < 0, -code, code).astype(BF16)


def decode(box, top):
    rows = box.shape[0]
    code = box[...].astype(F32)
    root = jnp.log(jnp.abs(code)) * (1.0 / (SPAN * math.log(2.0))) - LOW / SPAN
    size = ((root * root).reshape(rows // 8, 8, 128) * top[None]).reshape(rows, 128)
    return jnp.where(code < 0, -size, size)


def kernel(
    act, grad, q_in, q_out, out,
    a, q, part, sent_x, got_x, sent_y, got_y, tops, mine, theirs,
    load_sem, a_send, a_recv, z_send, z_recv, core_send, core_recv,
    send_x_sem, recv_x_sem, send_y_sem, recv_y_sem, end_send, end_recv,
):
    box_x, box_y = (sent_x, got_x, send_x_sem, recv_x_sem), (sent_y, got_y, send_y_sem, recv_y_sem)
    z, t = lax.axis_index("dp"), lax.axis_index("tensor")
    core, x, y = t % 2, (t // 2) % 4, t // 8
    tokens, w_in = act.shape
    w_out = grad.shape[1]
    half, wide = tokens // 2, w_in + w_out
    rx, ry = ROWS_X, half // 2 - ROWS_X

    def at(dx=0, dy=0, dz=0, other=False):
        index = (((y + dy + 4) % 4) * 4 + (x + dx + 4) % 4) * 2 + ((1 - core) if other else core)
        return ((z + dz + 4) % 4, index)

    own, partner_rows = core * half, (1 - core) * half

    loads = [
        pltpu.make_async_copy(act.at[pl.ds(own, half), :], a.at[:, pl.ds(0, w_in)], load_sem.at[0]),
        pltpu.make_async_copy(grad.at[pl.ds(own, half), :], a.at[:, pl.ds(w_in, w_out)], load_sem.at[1]),
    ]
    for j, step in enumerate(ORDER):
        columns = pl.ds(pl.multiple_of(((x + step) % 4) * 128, 128), 128)
        loads.append(pltpu.make_async_copy(q_in.at[:, columns], q.at[j, z, pl.ds(0, w_in), :], load_sem.at[2 + 2 * j]))
        loads.append(pltpu.make_async_copy(q_out.at[:, columns], q.at[j, z, pl.ds(w_in, w_out), :], load_sem.at[3 + 2 * j]))
    for load in loads:
        load.start()

    barrier = pltpu.get_barrier_semaphore()
    for device in (at(dx=1), at(dx=-1), at(dy=1), at(dy=-1), at(dz=1), at(dz=-1), at(other=True)):
        pl.semaphore_signal(barrier, inc=1, device_id=device, device_id_type=MESH)
    pl.semaphore_wait(barrier, 7)

    def copy(src, dst, send, recv, device):
        return pltpu.make_async_remote_copy(
            src_ref=src, dst_ref=dst, send_sem=send, recv_sem=recv, device_id=device, device_id_type=MESH)

    swaps = []
    for k, (low, count) in enumerate(((0, 2 * rx), (2 * rx, 2 * ry))):
        theirs_now = pl.ds(pl.multiple_of(partner_rows + low, 32), count)
        for h, (source, base, width) in enumerate(((act, wide, w_in), (grad, wide + w_in, w_out))):
            swaps.append(copy(source.at[theirs_now, :], a.at[pl.ds(low, count), pl.ds(base, width)],
                              a_send.at[2 * k + h], a_recv.at[2 * k + h], at(other=True)))

    def z_copy(j, kind):
        piece, low, count, dz = {
            0: (z, 0, wide, 1),
            1: (z, 0, wide, -1),
            2: ((z + 3) % 4, 0, wide // 2, 1),
            3: ((z + 1) % 4, wide // 2, wide // 2, -1),
        }[kind]
        ref = q.at[j, piece, pl.ds(low, count), :]
        return copy(ref, ref, z_send.at[j, kind], z_recv.at[j, kind], at(dz=dz))

    def z_arrival(j, kind):
        piece, low, count, dz = {
            0: ((z + 3) % 4, 0, wide, 1),
            1: ((z + 1) % 4, 0, wide, -1),
            2: ((z + 2) % 4, 0, wide // 2, 1),
            3: ((z + 2) % 4, wide // 2, wide // 2, -1),
        }[kind]
        ref = q.at[j, piece, pl.ds(low, count), :]
        return copy(ref, ref, z_send.at[j, kind], z_recv.at[j, kind], at(dz=dz))

    def core_copy(j, step):
        piece = (z + step) % 4
        return copy(q.at[j, piece, pl.ds(0, wide), :], q.at[j, piece, pl.ds(wide, wide), :],
                    core_send.at[j, step], core_recv.at[j, step], at(other=True))

    for j in range(4):
        loads[2 + 2 * j].wait()
        loads[3 + 2 * j].wait()
        if j < 2:
            z_copy(j, 0).start()
            z_copy(j, 1).start()
        core_copy(j, 0).start()
        if j == 0:
            swaps[0].start()
            swaps[1].start()
    swaps[2].start()
    swaps[3].start()

    def pass_near(j):
        z_arrival(j, 0).wait_recv()
        z_copy(j, 2).start()
        core_copy(j, 3).start()
        z_arrival(j, 1).wait_recv()
        z_copy(j, 3).start()
        core_copy(j, 1).start()
        if j < 2:
            z_copy(j + 2, 0).start()
            z_copy(j + 2, 1).start()

    def pass_far(j):
        z_arrival(j, 2).wait_recv()
        z_arrival(j, 3).wait_recv()
        core_copy(j, 2).start()

    def project(pieces, first, count_of):
        block = count_of // 2

        @pl.loop(0, 2)
        def _(i):
            line = pl.ds(pl.multiple_of(first + i * block, 32), block)
            for h, (low, count) in enumerate(((0, w_in), (w_in, w_out))):
                total = None
                for base in (low, low + wide):
                    right = [q[j, (z + step) % 4, pl.ds(base, count), :] for j, step in pieces]
                    right = right[0] if len(right) == 1 else jnp.concatenate(right, axis=1)
                    term = jnp.dot(a[line, pl.ds(base, count)], right, preferred_element_type=F32)
                    total = term if total is None else total + term
                for k, (j, step) in enumerate(pieces):
                    part[j, (z + step) % 4, h, line, :] = total[:, k * 128:(k + 1) * 128]

    def message(box, m, device):
        sent, got, out_sem, in_sem = box
        return copy(sent.at[m], got.at[m], out_sem.at[m], in_sem.at[m], device)

    def arrived(box, m):
        message(box, m, at(dx=1)).wait_recv()

    def read(box, m, h):
        got = box[1]
        r = (got.shape[1] - 16) // 2
        top = got[m, pl.ds(2 * r, 16), :].astype(F32).reshape(2, 8, 128)
        return decode(got.at[m, pl.ds(pl.multiple_of(h * r, 16), r), :], jnp.where(h == 0, top[0], top[1]))

    def send(box, m, source, device, add=None):
        sent = box[0]
        r = (sent.shape[1] - 16) // 2
        if add is not None:
            arrived(box, add)

        @pl.loop(0, 2)
        def _(h):
            value = source[h]
            if add is not None:
                value = value + read(box, add, h)
            encode(value, sent.at[m, pl.ds(pl.multiple_of(h * r, 16), r), :], tops.at[h])

        sent[m, pl.ds(2 * r, 16), :] = tops[...].reshape(16, 128).astype(BF16)
        message(box, m, device).start()

    def finish(box, target, first, second):
        arrived(box, first)
        arrived(box, second)

        @pl.loop(0, 2)
        def _(h):
            target[h] = target[h] + read(box, first, h) + read(box, second, h)

    def x_part(j, n, b):
        return part.at[j, n, :, pl.ds(pl.multiple_of(b * rx, 32), rx), :]

    def y_part(j, n, b):
        return part.at[j, n, :, pl.ds(pl.multiple_of(2 * rx + b * ry, 32), ry), :]

    def way_x(kind):
        return at(dx=jnp.where(kind < 3, 1, -1))

    def way_y(kind):
        return at(dy=jnp.where(kind < 3, 1, -1))

    def over_y(step, i, box, slot, source):
        n = (z + i) % 4
        role = (n - y + 4) % 4
        if step == 0:
            @pl.loop(0, jnp.where(role == 2, 2, jnp.where(role == 0, 0, 1)))
            def _(k):
                kind = jnp.where(role == 2, 3 * k, jnp.where(role == 1, 2, 5))
                b = jnp.where(role == 2, k, jnp.where(role == 1, 1, 0))
                send(box, slot(kind), source(n, b), way_y(kind))
        elif step == 1:
            @pl.when(role % 2 == 1)
            def _():
                kind = jnp.where(role == 1, 1, 4)
                send(box, slot(kind), source(n, role // 2), way_y(kind), add=slot(kind - 1))
        else:
            @pl.when(role == 0)
            def _():
                @pl.loop(0, 2)
                def _(b):
                    finish(box, source(n, b), slot(1 + 3 * b), slot(5 - 3 * b))

    here = set()

    def own_rows(k):
        if k not in here:
            here.add(k)
            if k == 0:
                loads[0].wait()
                loads[1].wait()
            swaps[2 * k].wait_recv()
            swaps[2 * k + 1].wait_recv()

    def pieces_at(pieces):
        for j, i in pieces:
            core_copy(j, i).wait_recv()
        return pieces

    def task(name, *index):
        k = index[0]
        if name == "near":
            pass_near(k)
        elif name == "far":
            pass_far(k)
        elif name == "own":
            pieces = [(2 * (k % 2), 0), (2 * (k % 2) + 1, 0)]
            own_rows(0)
            if k < 2:
                project(pieces_at(pieces), 0, 2 * rx)
            else:
                own_rows(1)
                project(pieces, 2 * rx, 2 * ry)
        elif name in ("pn", "pf"):
            own_rows(0)
            own_rows(1)
            project(pieces_at([(k, 3), (k, 1)] if name == "pn" else [(k, 2)]), 0, half)
        elif name == "xr":
            i = index[1]
            n = (z + i) % 4
            if k == 2:
                @pl.loop(0, 2)
                def _(b):
                    send(box_x, 12 * b + n, x_part(0, n, b), way_x(3 * b))
            elif k == 1:
                send(box_x, 8 + n, x_part(1, n, 1), right)
            else:
                send(box_x, 20 + n, x_part(2, n, 0), left)
        elif name == "xa":
            n = (z + index[1]) % 4
            if k == 1:
                send(box_x, 4 + n, x_part(1, n, 0), right, add=n)
            else:
                send(box_x, 16 + n, x_part(2, n, 1), left, add=12 + n)
        elif name == "xf":
            n = (z + k) % 4

            @pl.loop(0, 2)
            def _(b):
                finish(box_x, x_part(3, n, b), 4 + 12 * b + n, 20 - 12 * b + n)
        elif name == "y":
            j, i = index[1:]
            over_y(k, i, box_y, lambda kind: 4 * kind + j, lambda n, b: y_part(j, n, b))
        elif name == "ly":
            over_y(k, index[1], box_x, lambda kind: 24 + kind, lambda n, b: x_part(3, n, b))
        elif k == 0:
            @pl.loop(0, 2)
            def _(b):
                send(box_y, 24 + 3 * b, y_part(0, y, b), way_x(3 * b))
        elif k == 2:
            send(box_y, 26, y_part(1, y, 1), right)
        elif k == 5:
            send(box_y, 29, y_part(2, y, 0), left)
        elif k == 1:
            send(box_y, 25, y_part(1, y, 0), right, add=24)
        elif k == 4:
            send(box_y, 28, y_part(2, y, 1), left, add=27)
        else:
            @pl.loop(0, 2)
            def _(b):
                finish(box_y, y_part(3, y, b), 25 + 3 * b, 29 - 3 * b)

    right, left = at(dx=1), at(dx=-1)
    for name, *index in TASKS:
        task(name, *index)

    query = lax.broadcasted_iota(jnp.int32, (8, 128), 0)
    owner = lax.broadcasted_iota(jnp.int32, (8, 128), 1) // R

    def pick(which):
        return jnp.where((owner == query + 2 * which) & (query < 2), 1.0, 0.0).astype(BF16)

    rows = half // 4
    for g in range(4):
        line = pl.ds(g * rows, rows)
        product = part[3, y, 0, line, :] * part[3, y, 1, line, :] * (1.0 / math.sqrt(R))
        high = product.astype(BF16)
        rest = product - high.astype(F32)
        middle = rest.astype(BF16)
        low = (rest - middle.astype(F32)).astype(BF16)
        for which, target in ((core, mine), (1 - core, theirs)):
            mask = pick(which)
            total = None
            for term in (low, middle, high):
                s = lax.dot_general(mask, term, (((1,), (1,)), ((), ())), preferred_element_type=F32)
                total = s if total is None else total + s
            target[0, :, pl.ds(g * rows, rows)] = total
    final = copy(theirs.at[0], theirs.at[1], end_send, end_recv, at(other=True))
    final.start()
    out[:, pl.ds(pl.multiple_of(own, half), half)] = mine[0, pl.ds(0, 2), :]
    final.wait_recv()
    out[:, pl.ds(pl.multiple_of(partner_rows, half), half)] = theirs[1, pl.ds(0, 2), :]

    final.wait_send()
    for swap in swaps:
        swap.wait_send()
    for j in range(4):
        for k in range(4):
            z_copy(j, k).wait_send()
            core_copy(j, k).wait_send()

    @pl.loop(0, 30)
    def _(m):
        message(box_x, m, right).wait_send()
        message(box_y, m, right).wait_send()


def scores_of(act, grad, q_in, q_out):
    tokens, w_in = act.shape
    w_out = grad.shape[1]
    half, wide = tokens // 2, w_in + w_out
    rx, ry = ROWS_X, half // 2 - ROWS_X
    dma = pltpu.SemaphoreType.DMA
    scores = pl.pallas_call(
        kernel,
        out_shape=jax.ShapeDtypeStruct((2, tokens), F32),
        in_specs=[pl.BlockSpec(memory_space=pl.ANY)] * 4,
        out_specs=pl.BlockSpec(memory_space=pltpu.VMEM),
        scratch_shapes=[
            pltpu.VMEM((half, 2 * wide), BF16),
            pltpu.VMEM((4, 4, 2 * wide, 128), BF16),
            pltpu.VMEM((4, 4, 2, half, 128), F32),
            pltpu.VMEM((30, 2 * rx + 16, 128), BF16),
            pltpu.VMEM((30, 2 * rx + 16, 128), BF16),
            pltpu.VMEM((30, 2 * ry + 16, 128), BF16),
            pltpu.VMEM((30, 2 * ry + 16, 128), BF16),
            pltpu.VMEM((2, 8, 128), F32),
            pltpu.VMEM((1, 8, half), F32),
            pltpu.VMEM((2, 8, half), F32),
            dma((10,)), dma((4,)), dma((4,)),
            dma((4, 4)), dma((4, 4)), dma((4, 4)), dma((4, 4)),
            dma((30,)), dma((30,)), dma((30,)), dma((30,)), dma, dma,
        ],
        compiler_params=pltpu.CompilerParams(
            collective_id=0, has_side_effects=True, vmem_limit_bytes=58 * 1024 * 1024),
        cost_estimate=pl.CostEstimate(flops=2 * tokens * wide * 2048, bytes_accessed=6 * 2**20, transcendentals=0),
    )(act, grad, q_in, q_out)
    return scores.T


def solution(mesh):
    return jax.shard_map(
        scores_of,
        mesh=mesh,
        in_specs=(P("dp", "tensor"), P("dp", "tensor"), P("tensor", "dp"), P("tensor", "dp")),
        out_specs=P("dp", "tensor"),
        check_vma=False,
    )
```

time: 83.7 us -> 77.7 us (0.928)
  the two profiles are of different devices: /device:TPU:1 before, /device:TPU:17 now
where the time goes in v3:
time: 77.7 us; the launch traced here: 77.5 us
  Pallas kernels  76.2 us (98%)
  local copies, waits for them, and re-layouts  1.32 us (2%)
    pallas_call x1, Pallas kernels, scores_of(): pl.pallas_call(kernel, out_shape=jax.ShapeDtypeStruct((2, tokens), F32),...  76.2 us

profile of v3, /device:TPU:17, one launch (start us, length us, event | category | flops | bytes accessed | tf_op | source)
XLA Modules:
  0.0 77.5 jit_solution(12549267244396281773)
XLA Ops:
  0.0 76.2 %shard_map.46 = f32[2,2048]{1,0:T(2,128)} custom-call(bf16[2048,256]{1,0:T(8,128)(2,1)} %act.1, bf16[2048,896]{1,0:T(8,128)(2,1)} %grad.1, bf16[256,512]{1,0:T(8,128)(2,1)} %q_in.1, bf16[896,512]{1,0:T(8,128)(2,1)} %q_out.1), custom_call_target="tpu_custom_call" | custom-call | flops 9663676416 | bytes 6291456 | tf_op jit(solution)/shard_map/pallas_call | solution.py:372
  76.2 1.3 %copy.6 = f32[2048,2]{0,1:T(2,128)} copy(f32[2048,2]{0,1:T(2,128)} %bitcast.1) | data formatting | bytes 32768

commit v4 on v3

v4 whole, which is shorter than its diff:
```python
import functools
import math

import jax
import jax.numpy as jnp
from jax import lax
from jax.experimental import pallas as pl
from jax.experimental.pallas import tpu as pltpu
from jax.sharding import PartitionSpec as P

R = 32
MESH = pl.DeviceIdType.MESH
BF16, F32 = jnp.bfloat16, jnp.float32
SPAN, LOW = 250.0, -124.0
ORDER = (2, 1, 3, 0)
ROWS_X = (320, 224, 352, 224)
CUTS = 2
TASKS = (
    ('own', 0), ('own', 1), ('z', 1), ('xr', 2, 0), ('own', 3), ('own', 2), ('y', 0, 1, 0), ('near', 0),
    ('y', 0, 2, 0), ('xr', 3, 0), ('xr', 1, 0), ('pass', 0), ('pn', 0), ('y', 0, 0, 1), ('y', 0, 0, 3), ('xr', 2, 1),
    ('near', 1), ('z', 2), ('xa', 3, 0), ('xr', 2, 3), ('xa', 1, 0), ('pn', 1), ('y', 0, 1, 1), ('y', 0, 1, 3),
    ('y', 1, 1, 0), ('far', 0), ('pf', 0), ('pass', 1), ('y', 1, 2, 0), ('y', 0, 0, 2), ('y', 1, 0, 3),
    ('y', 0, 0, 0), ('xr', 2, 2), ('y', 1, 0, 1), ('near', 2), ('xa', 1, 1), ('pass', 2), ('z', 3), ('y', 1, 1, 3),
    ('y', 1, 0, 2), ('xa', 1, 3), ('y', 1, 1, 1), ('pn', 2), ('xr', 3, 3), ('xf', 0), ('xr', 3, 1), ('y', 0, 3, 0),
    ('y', 0, 2, 3), ('xr', 1, 1), ('y', 0, 2, 1), ('far', 1), ('far', 2), ('y', 2, 0, 3), ('xa', 3, 1), ('pf', 1),
    ('y', 2, 2, 0), ('xa', 3, 3), ('y', 0, 1, 2), ('xr', 1, 2), ('y', 1, 0, 0), ('pf', 2), ('y', 0, 2, 2),
    ('y', 1, 2, 1), ('ly', 0, 0, 1), ('y', 2, 0, 1), ('xr', 1, 3), ('y', 2, 0, 2), ('near', 3), ('y', 1, 1, 2),
    ('y', 1, 2, 3), ('xa', 3, 2), ('pass', 3), ('y', 1, 3, 0), ('y', 2, 0, 0), ('xa', 1, 2), ('y', 1, 2, 2),
    ('pn', 3), ('y', 0, 3, 1), ('y', 0, 3, 3), ('xr', 3, 2), ('lx', 0), ('xf', 1), ('ly', 0, 1, 1), ('far', 3),
    ('xf', 3), ('ly', 0, 3, 0), ('ly', 0, 1, 0), ('y', 2, 2, 1), ('ly', 0, 3, 1), ('ly', 0, 0, 0), ('y', 2, 2, 2),
    ('pf', 3), ('y', 2, 1, 2), ('y', 2, 1, 0), ('y', 0, 3, 2), ('y', 2, 1, 3), ('ly', 1, 1, 1), ('y', 2, 1, 1),
    ('ly', 1, 3, 1), ('xf', 2), ('ly', 0, 2, 0), ('ly', 0, 2, 1), ('y', 1, 3, 1), ('ly', 1, 0, 1), ('y', 2, 2, 3),
    ('y', 1, 3, 2), ('lx', 4), ('y', 1, 3, 3), ('lx', 2), ('ly', 1, 0, 0), ('y', 2, 3, 0), ('ly', 2, 3, 1), ('lx', 1),
    ('ly', 1, 1, 0), ('ly', 1, 2, 0), ('ly', 1, 3, 0), ('lx', 5), ('ly', 1, 2, 1), ('ly', 2, 0, 0), ('ly', 2, 0, 1),
    ('y', 2, 3, 1), ('ly', 2, 2, 0), ('ly', 2, 1, 1), ('y', 2, 3, 3), ('y', 2, 3, 2), ('lx', 9), ('ly', 2, 1, 0),
    ('ly', 2, 3, 0), ('ly', 2, 2, 1),
)


def encode(value, box, top_box):
    rows = value.shape[0]
    size = jnp.abs(value).reshape(rows // 8, 8, 128)
    top = jnp.max(size, axis=0).astype(BF16).astype(F32)
    top_box[...] = top
    part = size * (1.0 / jnp.maximum(top, 1e-30))[None]
    root = part * lax.rsqrt(part + 1e-30)
    code = jnp.exp2(root * SPAN + LOW).reshape(rows, 128)
    box[...] = jnp.where(value < 0, -code, code).astype(BF16)


def decode(box, top):
    rows = box.shape[0]
    code = box[...].astype(F32)
    root = jnp.log(jnp.abs(code)) * (1.0 / (SPAN * math.log(2.0))) - LOW / SPAN
    size = ((root * root).reshape(rows // 8, 8, 128) * top[None]).reshape(rows, 128)
    return jnp.where(code < 0, -size, size)


def kernel(
    act, grad, q_in, q_out, out,
    a, q, part, sent_x, got_x, sent_y, got_y, tops, mine, theirs,
    load_sem, a_send, a_recv, z_send, z_recv, core_send, core_recv,
    send_x_sem, recv_x_sem, send_y_sem, recv_y_sem, end_send, end_recv,
):
    box_x, box_y = (sent_x, got_x, send_x_sem, recv_x_sem), (sent_y, got_y, send_y_sem, recv_y_sem)
    z, t = lax.axis_index("dp"), lax.axis_index("tensor")
    core, x, y = t % 2, (t // 2) % 4, t // 8
    tokens, w_in = act.shape
    w_out = grad.shape[1]
    half, wide = tokens // 2, w_in + w_out
    rows_x = ROWS_X
    rows_y = tuple(half // 2 - r for r in ROWS_X)

    def at(dx=0, dy=0, dz=0, other=False):
        index = (((y + dy + 4) % 4) * 4 + (x + dx + 4) % 4) * 2 + ((1 - core) if other else core)
        return ((z + dz + 4) % 4, index)

    own, partner_rows = core * half, (1 - core) * half

    barrier = pltpu.get_barrier_semaphore()
    for device in (at(dx=1), at(dx=-1), at(dy=1), at(dy=-1), at(dz=1), at(dz=-1), at(other=True)):
        pl.semaphore_signal(barrier, inc=1, device_id=device, device_id_type=MESH)

    loads = [
        pltpu.make_async_copy(act.at[pl.ds(own, half), :], a.at[:, pl.ds(0, w_in)], load_sem.at[0]),
        pltpu.make_async_copy(grad.at[pl.ds(own, half), :], a.at[:, pl.ds(w_in, w_out)], load_sem.at[1]),
    ]
    for j, step in enumerate(ORDER):
        columns = pl.ds(pl.multiple_of(((x + step) % 4) * 128, 128), 128)
        loads.append(pltpu.make_async_copy(q_in.at[:, columns], q.at[j, z, pl.ds(0, w_in), :], load_sem.at[2 + 2 * j]))
        loads.append(pltpu.make_async_copy(q_out.at[:, columns], q.at[j, z, pl.ds(w_in, w_out), :], load_sem.at[3 + 2 * j]))
    for load in loads:
        load.start()

    pl.semaphore_wait(barrier, 7)

    def copy(src, dst, send, recv, device):
        return pltpu.make_async_remote_copy(
            src_ref=src, dst_ref=dst, send_sem=send, recv_sem=recv, device_id=device, device_id_type=MESH)

    swaps = []
    for k, (low, count) in enumerate(((0, 2 * rows_x[0]), (2 * rows_x[0], 2 * rows_y[0]))):
        theirs_now = pl.ds(pl.multiple_of(partner_rows + low, 32), count)
        for h, (source, base, width) in enumerate(((act, wide, w_in), (grad, wide + w_in, w_out))):
            swaps.append(copy(source.at[theirs_now, :], a.at[pl.ds(low, count), pl.ds(base, width)],
                              a_send.at[2 * k + h], a_recv.at[2 * k + h], at(other=True)))

    def z_copy(j, kind):
        piece, low, count, dz = {
            0: (z, 0, wide, 1),
            1: (z, 0, wide, -1),
            2: ((z + 3) % 4, 0, wide // 2, 1),
            3: ((z + 1) % 4, wide // 2, wide // 2, -1),
        }[kind]
        ref = q.at[j, piece, pl.ds(low, count), :]
        return copy(ref, ref, z_send.at[j, kind], z_recv.at[j, kind], at(dz=dz))

    def z_arrival(j, kind):
        piece, low, count, dz = {
            0: ((z + 3) % 4, 0, wide, 1),
            1: ((z + 1) % 4, 0, wide, -1),
            2: ((z + 2) % 4, 0, wide // 2, 1),
            3: ((z + 2) % 4, wide // 2, wide // 2, -1),
        }[kind]
        ref = q.at[j, piece, pl.ds(low, count), :]
        return copy(ref, ref, z_send.at[j, kind], z_recv.at[j, kind], at(dz=dz))

    def core_copy(j, step):
        piece = (z + step) % 4
        return copy(q.at[j, piece, pl.ds(0, wide), :], q.at[j, piece, pl.ds(wide, wide), :],
                    core_send.at[j, step], core_recv.at[j, step], at(other=True))

    for j in range(4):
        loads[2 + 2 * j].wait()
        loads[3 + 2 * j].wait()
        if j == 0:
            z_copy(j, 0).start()
            z_copy(j, 1).start()
        core_copy(j, 0).start()
        if j == 0:
            swaps[0].start()
            swaps[1].start()
    swaps[2].start()
    swaps[3].start()

    here = set()

    def near_here(j):
        if j not in here:
            here.add(j)
            z_arrival(j, 0).wait_recv()
            z_arrival(j, 1).wait_recv()

    def project(pieces, first, count_of):
        block = count_of // 2

        @pl.loop(0, 2)
        def _(i):
            line = pl.ds(pl.multiple_of(first + i * block, 32), block)
            for h, (low, count) in enumerate(((0, w_in), (w_in, w_out))):
                total = None
                for base in (low, low + wide):
                    right = [q[j, (z + step) % 4, pl.ds(base, count), :] for j, step in pieces]
                    right = right[0] if len(right) == 1 else jnp.concatenate(right, axis=1)
                    term = jnp.dot(a[line, pl.ds(base, count)], right, preferred_element_type=F32)
                    total = term if total is None else total + term
                for k, (j, step) in enumerate(pieces):
                    part[j, (z + step) % 4, h, line, :] = total[:, k * 128:(k + 1) * 128]

    def message(box, m, device, r):
        sent, got, out_sem, in_sem = box
        line = pl.ds(0, 2 * r + 16)
        return copy(sent.at[m, line, :], got.at[m, line, :], out_sem.at[m], in_sem.at[m], device)

    def arrived(box, m, r):
        message(box, m, at(dx=1), r).wait_recv()

    def left_box(box, m, r):
        message(box, m, at(dx=1), r).wait_send()

    def read(box, m, h, r):
        got = box[1]
        top = got[m, pl.ds(2 * r, 16), :].astype(F32).reshape(2, 8, 128)
        return decode(got.at[m, pl.ds(pl.multiple_of(h * r, 16), r), :], jnp.where(h == 0, top[0], top[1]))

    def send(box, m, source, device, add=None):
        sent, r = box[0], source.shape[1]
        if add is not None:
            arrived(box, add, r)

        @pl.loop(0, 2)
        def _(h):
            value = source[h]
            if add is not None:
                value = value + read(box, add, h, r)
            encode(value, sent.at[m, pl.ds(pl.multiple_of(h * r, 16), r), :], tops.at[h])

        sent[m, pl.ds(2 * r, 16), :] = tops[...].reshape(16, 128).astype(BF16)
        message(box, m, device, r).start()

    def finish(box, target, first, second):
        r = target.shape[1]
        arrived(box, first, r)
        arrived(box, second, r)

        @pl.loop(0, 2)
        def _(h):
            target[h] = target[h] + read(box, first, h, r) + read(box, second, h, r)

    def x_part(j, i, b, c=0, cuts=1):
        r = rows_x[i]
        return part.at[j, (z + i) % 4, :, pl.ds(pl.multiple_of(b * r + c * (r // cuts), 16), r // cuts), :]

    def y_part(j, i, b):
        r = rows_y[i]
        return part.at[j, (z + i) % 4, :, pl.ds(pl.multiple_of(2 * rows_x[i] + b * r, 16), r), :]

    def way_x(kind):
        return at(dx=jnp.where(kind < 3, 1, -1))

    def way_y(kind):
        return at(dy=jnp.where(kind < 3, 1, -1))

    def over_y(step, i, box, slot, source):
        role = (z + i - y + 4) % 4
        if step == 0:
            @pl.loop(0, jnp.where(role == 2, 2, jnp.where(role == 0, 0, 1)))
            def _(k):
                kind = jnp.where(role == 2, 3 * k, jnp.where(role == 1, 2, 5))
                b = jnp.where(role == 2, k, jnp.where(role == 1, 1, 0))
                send(box, slot(kind), source(b), way_y(kind))
        elif step == 1:
            @pl.when(role % 2 == 1)
            def _():
                kind = jnp.where(role == 1, 1, 4)
                send(box, slot(kind), source(role // 2), way_y(kind), add=slot(kind - 1))
        else:
            @pl.when(role == 0)
            def _():
                @pl.loop(0, 2)
                def _(b):
                    finish(box, source(b), slot(1 + 3 * b), slot(5 - 3 * b))

    def over_y_left(i, box, slot, r):
        role = (z + i - y + 4) % 4

        @pl.when(role == 2)
        def _():
            left_box(box, slot(0), r)
            left_box(box, slot(3), r)

        @pl.when(role % 2 == 1)
        def _():
            kind = jnp.where(role == 1, 1, 4)
            left_box(box, slot(kind), r)
            left_box(box, slot(kind + 1), r)

    def own_place(body):
        for i in range(4):
            @pl.when((y - z + 4) % 4 == i)
            def _(i=i):
                body(i)

    def own_rows(k):
        if ("rows", k) not in here:
            here.add(("rows", k))
            if k == 0:
                loads[0].wait()
                loads[1].wait()
            swaps[2 * k].wait_recv()
            swaps[2 * k + 1].wait_recv()

    def pieces_at(pieces):
        for j, i in pieces:
            core_copy(j, i).wait_recv()
        return pieces

    def last_x(k, i):
        if k == 0:
            @pl.loop(0, 2)
            def _(b):
                send(box_y, 24 + 3 * b, y_part(0, i, b), way_x(3 * b))
        elif k == 2:
            send(box_y, 26, y_part(1, i, 1), right)
        elif k == 5:
            send(box_y, 29, y_part(2, i, 0), left)
        elif k == 1:
            send(box_y, 25, y_part(1, i, 0), right, add=24)
        elif k == 4:
            send(box_y, 28, y_part(2, i, 1), left, add=27)
        else:
            @pl.loop(0, 2)
            def _(b):
                finish(box_y, y_part(3, i, b), 25 + 3 * b, 29 - 3 * b)

    def task(name, *index):
        k = index[0]
        if name == "z":
            if k >= 2:
                near_here(k - 2)
            z_copy(k, 0).start()
            z_copy(k, 1).start()
        elif name == "pass":
            near_here(k)
            z_copy(k, 2).start()
            z_copy(k, 3).start()
        elif name == "near":
            near_here(k)
            core_copy(k, 3).start()
            core_copy(k, 1).start()
        elif name == "far":
            z_arrival(k, 2).wait_recv()
            z_arrival(k, 3).wait_recv()
            core_copy(k, 2).start()
        elif name == "own":
            pieces = [(2 * (k % 2), 0), (2 * (k % 2) + 1, 0)]
            own_rows(0)
            if k < 2:
                project(pieces_at(pieces), 0, 2 * rows_x[0])
            else:
                own_rows(1)
                project(pieces, 2 * rows_x[0], 2 * rows_y[0])
        elif name in ("pn", "pf"):
            own_rows(0)
            own_rows(1)
            project(pieces_at([(k, 3), (k, 1)] if name == "pn" else [(k, 2)]), 0, half)
        elif name == "xr":
            i = index[1]
            n = (z + i) % 4
            if k == 2:
                @pl.loop(0, 2)
                def _(b):
                    send(box_x, 12 * b + n, x_part(0, i, b), way_x(3 * b))
            elif k == 1:
                send(box_x, 8 + n, x_part(1, i, 1), right)
            else:
                send(box_x, 20 + n, x_part(2, i, 0), left)
        elif name == "xa":
            i = index[1]
            n = (z + i) % 4
            if k == 1:
                send(box_x, 4 + n, x_part(1, i, 0), right, add=n)
            else:
                send(box_x, 16 + n, x_part(2, i, 1), left, add=12 + n)
        elif name == "xf":
            n = (z + k) % 4

            @pl.loop(0, 2)
            def _(b):
                finish(box_x, x_part(3, k, b), 4 + 12 * b + n, 20 - 12 * b + n)
        elif name == "y":
            j, i = index[1:]
            over_y(k, i, box_y, lambda kind: 4 * kind + j, lambda b: y_part(j, i, b))
        elif name == "ly":
            i, c = index[1:]
            over_y(k, i, box_x, lambda kind: 24 + 6 * c + kind, lambda b: x_part(3, i, b, c, CUTS))
        else:
            own_place(functools.partial(last_x, k))

    right, left = at(dx=1), at(dx=-1)
    for name, *index in TASKS:
        task(name, *index)

    query = lax.broadcasted_iota(jnp.int32, (8, 128), 0)
    owner = lax.broadcasted_iota(jnp.int32, (8, 128), 1) // R

    mask = jnp.concatenate([
        jnp.where((owner == query + 2 * which) & (query < 2), 1.0, 0.0).astype(BF16) for which in (core, 1 - core)], axis=0)
    rows = half // 4
    for g in range(4):
        line = pl.ds(g * rows, rows)
        product = part[3, y, 0, line, :] * part[3, y, 1, line, :] * (1.0 / math.sqrt(R))
        high = product.astype(BF16)
        rest = product - high.astype(F32)
        middle = rest.astype(BF16)
        low = (rest - middle.astype(F32)).astype(BF16)
        total = None
        for term in (low, middle, high):
            s = lax.dot_general(mask, term, (((1,), (1,)), ((), ())), preferred_element_type=F32)
            total = s if total is None else total + s
        mine[0, :, line] = total[:8]
        theirs[0, :, line] = total[8:]
    final = copy(theirs.at[0], theirs.at[1], end_send, end_recv, at(other=True))
    final.start()
    out[:, pl.ds(pl.multiple_of(own, half), half)] = mine[0, pl.ds(0, 2), :]
    final.wait_recv()
    out[:, pl.ds(pl.multiple_of(partner_rows, half), half)] = theirs[1, pl.ds(0, 2), :]

    final.wait_send()
    for swap in swaps:
        swap.wait_send()
    for j in range(4):
        for k in range(4):
            z_copy(j, k).wait_send()
            core_copy(j, k).wait_send()

    for i in range(4):
        @pl.loop(0, 6)
        def _(kind):
            left_box(box_x, kind * 4 + (z + i) % 4, rows_x[i])

        @pl.loop(0, 4)
        def _(j):
            over_y_left(i, box_y, lambda kind: 4 * kind + j, rows_y[i])

        for c in range(CUTS):
            over_y_left(i, box_x, lambda kind: 24 + 6 * c + kind, rows_x[i] // CUTS)

    def last_left(i):
        @pl.loop(0, 6)
        def _(kind):
            left_box(box_y, 24 + kind, rows_y[i])

    own_place(last_left)


def scores_of(act, grad, q_in, q_out):
    tokens, w_in = act.shape
    w_out = grad.shape[1]
    half, wide = tokens // 2, w_in + w_out
    rx, ry = max(ROWS_X), half // 2 - min(ROWS_X)
    slots = 24 + 6 * CUTS
    dma = pltpu.SemaphoreType.DMA
    scores = pl.pallas_call(
        kernel,
        out_shape=jax.ShapeDtypeStruct((2, tokens), F32),
        in_specs=[pl.BlockSpec(memory_space=pl.ANY)] * 4,
        out_specs=pl.BlockSpec(memory_space=pltpu.VMEM),
        scratch_shapes=[
            pltpu.VMEM((half, 2 * wide), BF16),
            pltpu.VMEM((4, 4, 2 * wide, 128), BF16),
            pltpu.VMEM((4, 4, 2, half, 128), F32),
            pltpu.VMEM((slots, 2 * rx + 16, 128), BF16),
            pltpu.VMEM((slots, 2 * rx + 16, 128), BF16),
            pltpu.VMEM((30, 2 * ry + 16, 128), BF16),
            pltpu.VMEM((30, 2 * ry + 16, 128), BF16),
            pltpu.VMEM((2, 8, 128), F32),
            pltpu.VMEM((1, 8, half), F32),
            pltpu.VMEM((2, 8, half), F32),
            dma((10,)), dma((4,)), dma((4,)),
            dma((4, 4)), dma((4, 4)), dma((4, 4)), dma((4, 4)),
            dma((slots,)), dma((slots,)), dma((30,)), dma((30,)), dma, dma,
        ],
        compiler_params=pltpu.CompilerParams(
            collective_id=0, has_side_effects=True, vmem_limit_bytes=58 * 1024 * 1024),
        cost_estimate=pl.CostEstimate(flops=2 * tokens * wide * 2048, bytes_accessed=6 * 2**20, transcendentals=0),
    )(act, grad, q_in, q_out)
    return scores.T


def solution(mesh):
    return jax.shard_map(
        scores_of,
        mesh=mesh,
        in_specs=(P("dp", "tensor"), P("dp", "tensor"), P("tensor", "dp"), P("tensor", "dp")),
        out_specs=P("dp", "tensor"),
        check_vma=False,
    )
```

time: 77.7 us -> 75.8 us (0.976)
  the two profiles are of different devices: /device:TPU:17 before, /device:TPU:9 now
where the time goes in v4:
time: 75.8 us; the launch traced here: 75.7 us
  Pallas kernels  74.3 us (98%)
  local copies, waits for them, and re-layouts  1.32 us (2%)
    pallas_call x1, Pallas kernels, scores_of(): pl.pallas_call(kernel, out_shape=jax.ShapeDtypeStruct((2, tokens), F32),...  74.3 us

profile of v4, /device:TPU:9, one launch (start us, length us, event | category | flops | bytes accessed | tf_op | source)
XLA Modules:
  0.0 75.7 jit_solution(5615588786019678613)
XLA Ops:
  0.0 74.3 %shard_map.46 = f32[2,2048]{1,0:T(2,128)} custom-call(bf16[2048,256]{1,0:T(8,128)(2,1)} %act.1, bf16[2048,896]{1,0:T(8,128)(2,1)} %grad.1, bf16[256,512]{1,0:T(8,128)(2,1)} %q_in.1, bf16[896,512]{1,0:T(8,128)(2,1)} %q_out.1), custom_call_target="tpu_custom_call" | custom-call | flops 9663676416 | bytes 6291456 | tf_op jit(solution)/shard_map/pallas_call | solution.py:424
  74.3 1.3 %copy.6 = f32[2048,2]{0,1:T(2,128)} copy(f32[2048,2]{0,1:T(2,128)} %bitcast.1) | data formatting | bytes 32768

commit v5 on v4

--- a/solution.py
+++ b/solution.py
@@ -14,26 +14,24 @@
 SPAN, LOW = 250.0, -124.0
 ORDER = (2, 1, 3, 0)
 ROWS_X = (320, 224, 352, 224)
-CUTS = 2
+CUTS = 1
 TASKS = (
-    ('own', 0), ('own', 1), ('z', 1), ('xr', 2, 0), ('own', 3), ('own', 2), ('y', 0, 1, 0), ('near', 0),
-    ('y', 0, 2, 0), ('xr', 3, 0), ('xr', 1, 0), ('pass', 0), ('pn', 0), ('y', 0, 0, 1), ('y', 0, 0, 3), ('xr', 2, 1),
-    ('near', 1), ('z', 2), ('xa', 3, 0), ('xr', 2, 3), ('xa', 1, 0), ('pn', 1), ('y', 0, 1, 1), ('y', 0, 1, 3),
-    ('y', 1, 1, 0), ('far', 0), ('pf', 0), ('pass', 1), ('y', 1, 2, 0), ('y', 0, 0, 2), ('y', 1, 0, 3),
-    ('y', 0, 0, 0), ('xr', 2, 2), ('y', 1, 0, 1), ('near', 2), ('xa', 1, 1), ('pass', 2), ('z', 3), ('y', 1, 1, 3),
-    ('y', 1, 0, 2), ('xa', 1, 3), ('y', 1, 1, 1), ('pn', 2), ('xr', 3, 3), ('xf', 0), ('xr', 3, 1), ('y', 0, 3, 0),
-    ('y', 0, 2, 3), ('xr', 1, 1), ('y', 0, 2, 1), ('far', 1), ('far', 2), ('y', 2, 0, 3), ('xa', 3, 1), ('pf', 1),
-    ('y', 2, 2, 0), ('xa', 3, 3), ('y', 0, 1, 2), ('xr', 1, 2), ('y', 1, 0, 0), ('pf', 2), ('y', 0, 2, 2),
-    ('y', 1, 2, 1), ('ly', 0, 0, 1), ('y', 2, 0, 1), ('xr', 1, 3), ('y', 2, 0, 2), ('near', 3), ('y', 1, 1, 2),
-    ('y', 1, 2, 3), ('xa', 3, 2), ('pass', 3), ('y', 1, 3, 0), ('y', 2, 0, 0), ('xa', 1, 2), ('y', 1, 2, 2),
-    ('pn', 3), ('y', 0, 3, 1), ('y', 0, 3, 3), ('xr', 3, 2), ('lx', 0), ('xf', 1), ('ly', 0, 1, 1), ('far', 3),
-    ('xf', 3), ('ly', 0, 3, 0), ('ly', 0, 1, 0), ('y', 2, 2, 1), ('ly', 0, 3, 1), ('ly', 0, 0, 0), ('y', 2, 2, 2),
-    ('pf', 3), ('y', 2, 1, 2), ('y', 2, 1, 0), ('y', 0, 3, 2), ('y', 2, 1, 3), ('ly', 1, 1, 1), ('y', 2, 1, 1),
-    ('ly', 1, 3, 1), ('xf', 2), ('ly', 0, 2, 0), ('ly', 0, 2, 1), ('y', 1, 3, 1), ('ly', 1, 0, 1), ('y', 2, 2, 3),
-    ('y', 1, 3, 2), ('lx', 4), ('y', 1, 3, 3), ('lx', 2), ('ly', 1, 0, 0), ('y', 2, 3, 0), ('ly', 2, 3, 1), ('lx', 1),
-    ('ly', 1, 1, 0), ('ly', 1, 2, 0), ('ly', 1, 3, 0), ('lx', 5), ('ly', 1, 2, 1), ('ly', 2, 0, 0), ('ly', 2, 0, 1),
-    ('y', 2, 3, 1), ('ly', 2, 2, 0), ('ly', 2, 1, 1), ('y', 2, 3, 3), ('y', 2, 3, 2), ('lx', 9), ('ly', 2, 1, 0),
-    ('ly', 2, 3, 0), ('ly', 2, 2, 1),
+    ('own', 0), ('xr', 2, 0), ('z', 1), ('own', 1), ('own', 2), ('near', 0), ('y', 0, 1, 0), ('y', 0, 0, 0),
+    ('xr', 1, 0), ('pass', 0), ('pn', 0), ('xa', 3, 0), ('xa', 1, 0), ('y', 0, 0, 3), ('xr', 3, 0), ('y', 0, 0, 1),
+    ('near', 1), ('z', 2), ('pass', 1), ('xr', 2, 3), ('pn', 1), ('y', 0, 1, 1), ('y', 0, 1, 3), ('y', 1, 1, 0),
+    ('far', 0), ('xr', 2, 1), ('y', 1, 0, 1), ('own', 3), ('xr', 1, 1), ('xr', 1, 3), ('y', 1, 0, 3), ('xf', 0),
+    ('pf', 0), ('y', 0, 0, 2), ('y', 0, 2, 0), ('near', 2), ('pass', 2), ('y', 1, 1, 3), ('xa', 1, 1), ('xr', 2, 2),
+    ('y', 1, 1, 1), ('z', 3), ('pn', 2), ('y', 0, 2, 3), ('y', 0, 2, 1), ('far', 1), ('xr', 3, 1), ('xa', 3, 1),
+    ('y', 2, 0, 3), ('y', 1, 0, 0), ('y', 1, 0, 2), ('far', 2), ('pf', 1), ('y', 0, 1, 2), ('pf', 2), ('y', 0, 2, 2),
+    ('xr', 3, 2), ('ly', 0, 0, 0), ('y', 2, 0, 1), ('xr', 1, 2), ('y', 1, 2, 3), ('y', 0, 3, 0), ('y', 1, 2, 1),
+    ('xa', 3, 2), ('pass', 3), ('near', 3), ('y', 1, 1, 2), ('y', 1, 2, 0), ('xa', 3, 3), ('xa', 1, 2),
+    ('y', 2, 0, 0), ('y', 1, 2, 2), ('pn', 3), ('y', 0, 3, 3), ('y', 0, 3, 1), ('far', 3), ('y', 2, 1, 1),
+    ('y', 2, 1, 2), ('xa', 1, 3), ('xr', 3, 3), ('y', 2, 1, 3), ('pf', 3), ('y', 0, 3, 2), ('xf', 1), ('xf', 2),
+    ('ly', 0, 2, 0), ('y', 2, 1, 0), ('y', 2, 2, 2), ('y', 2, 0, 2), ('ly', 1, 0, 0), ('y', 2, 2, 1), ('lx', 0),
+    ('y', 1, 3, 1), ('y', 1, 3, 3), ('lx', 2), ('y', 2, 2, 0), ('y', 2, 2, 3), ('ly', 0, 1, 0), ('lx', 5), ('xf', 3),
+    ('ly', 0, 3, 0), ('y', 1, 3, 2), ('lx', 4), ('lx', 1), ('ly', 1, 3, 0), ('y', 1, 3, 0), ('ly', 2, 0, 0),
+    ('ly', 1, 2, 0), ('ly', 1, 1, 0), ('left', 0), ('y', 2, 3, 3), ('y', 2, 3, 0), ('y', 2, 3, 2), ('y', 2, 3, 1),
+    ('lx', 9), ('ly', 2, 2, 0), ('ly', 2, 1, 0), ('ly', 2, 3, 0),
 )
 
 
@@ -42,9 +40,9 @@
     size = jnp.abs(value).reshape(rows // 8, 8, 128)
     top = jnp.max(size, axis=0).astype(BF16).astype(F32)
     top_box[...] = top
-    part = size * (1.0 / jnp.maximum(top, 1e-30))[None]
+    part = size * (SPAN * SPAN / jnp.maximum(top, 1e-30))[None]
     root = part * lax.rsqrt(part + 1e-30)
-    code = jnp.exp2(root * SPAN + LOW).reshape(rows, 128)
+    code = jnp.exp2(root + LOW).reshape(rows, 128)
     box[...] = jnp.where(value < 0, -code, code).astype(BF16)
 
 
@@ -158,12 +156,12 @@
         def _(i):
             line = pl.ds(pl.multiple_of(first + i * block, 32), block)
             for h, (low, count) in enumerate(((0, w_in), (w_in, w_out))):
-                total = None
-                for base in (low, low + wide):
-                    right = [q[j, (z + step) % 4, pl.ds(base, count), :] for j, step in pieces]
-                    right = right[0] if len(right) == 1 else jnp.concatenate(right, axis=1)
-                    term = jnp.dot(a[line, pl.ds(base, count)], right, preferred_element_type=F32)
-                    total = term if total is None else total + term
+                bases = (low, low + wide)
+                rows_of = jnp.concatenate([a[line, pl.ds(base, count)] for base in bases], axis=1)
+                columns = [
+                    jnp.concatenate([q[j, (z + step) % 4, pl.ds(base, count), :] for base in bases], axis=0) for j, step in pieces]
+                columns = columns[0] if len(columns) == 1 else jnp.concatenate(columns, axis=1)
+                total = jnp.dot(rows_of, columns, preferred_element_type=F32)
                 for k, (j, step) in enumerate(pieces):
                     part[j, (z + step) % 4, h, line, :] = total[:, k * 128:(k + 1) * 128]
 
@@ -255,6 +253,24 @@
             left_box(box, slot(kind), r)
             left_box(box, slot(kind + 1), r)
 
+    def sends_left(phases):
+        for i in range(4):
+            for j in phases:
+                over_y_left(i, box_y, lambda kind: 4 * kind + j, rows_y[i])
+
+    def early_left():
+        for swap in swaps:
+            swap.wait_send()
+        for j in range(4):
+            for k in range(4):
+                z_copy(j, k).wait_send()
+                core_copy(j, k).wait_send()
+        for i in range(4):
+            @pl.loop(0, 6)
+            def _(kind):
+                left_box(box_x, kind * 4 + (z + i) % 4, rows_x[i])
+        sends_left((0, 1, 2))
+
     def own_place(body):
         for i in range(4):
             @pl.when((y - z + 4) % 4 == i)
@@ -295,7 +311,9 @@
 
     def task(name, *index):
         k = index[0]
-        if name == "z":
+        if name == "left":
+            early_left()
+        elif name == "z":
             if k >= 2:
                 near_here(k - 2)
             z_copy(k, 0).start()
@@ -387,22 +405,8 @@
     out[:, pl.ds(pl.multiple_of(partner_rows, half), half)] = theirs[1, pl.ds(0, 2), :]
 
     final.wait_send()
-    for swap in swaps:
-        swap.wait_send()
-    for j in range(4):
-        for k in range(4):
-            z_copy(j, k).wait_send()
-            core_copy(j, k).wait_send()
-
+    sends_left((3,))
     for i in range(4):
-        @pl.loop(0, 6)
-        def _(kind):
-            left_box(box_x, kind * 4 + (z + i) % 4, rows_x[i])
-
-        @pl.loop(0, 4)
-        def _(j):
-            over_y_left(i, box_y, lambda kind: 4 * kind + j, rows_y[i])
-
         for c in range(CUTS):
             over_y_left(i, box_x, lambda kind: 24 + 6 * c + kind, rows_x[i] // CUTS)
 

time: 75.8 us -> 73.4 us (0.968)
  the two profiles are of different devices: /device:TPU:9 before, /device:TPU:1 now
where the time goes in v5:
time: 73.4 us; the launch traced here: 72.3 us
  Pallas kernels  71 us (97%)
  local copies, waits for them, and re-layouts  1.32 us (2%)
    pallas_call x1, Pallas kernels, scores_of(): pl.pallas_call(kernel, out_shape=jax.ShapeDtypeStruct((2, tokens), F32),...  71 us

profile of v5, /device:TPU:1, one launch (start us, length us, event | category | flops | bytes accessed | tf_op | source)
XLA Modules:
  0.0 72.3 jit_solution(2760191382347549279)
XLA Ops:
  0.0 71.0 %shard_map.46 = f32[2,2048]{1,0:T(2,128)} custom-call(bf16[2048,256]{1,0:T(8,128)(2,1)} %act.1, bf16[2048,896]{1,0:T(8,128)(2,1)} %grad.1, bf16[256,512]{1,0:T(8,128)(2,1)} %q_in.1, bf16[896,512]{1,0:T(8,128)(2,1)} %q_out.1), custom_call_target="tpu_custom_call" | custom-call | flops 9663676416 | bytes 6291456 | tf_op jit(solution)/shard_map/pallas_call | solution.py:428
  71.0 1.3 %copy.6 = f32[2048,2]{0,1:T(2,128)} copy(f32[2048,2]{0,1:T(2,128)} %bitcast.1) | data formatting | bytes 32768

commit v6 on v5

--- a/solution.py
+++ b/solution.py
@@ -13,25 +13,25 @@
 BF16, F32 = jnp.bfloat16, jnp.float32
 SPAN, LOW = 250.0, -124.0
 ORDER = (2, 1, 3, 0)
-ROWS_X = (320, 224, 352, 224)
+ROWS_X = (320, 224, 384, 224)
 CUTS = 1
 TASKS = (
-    ('own', 0), ('xr', 2, 0), ('z', 1), ('own', 1), ('own', 2), ('near', 0), ('y', 0, 1, 0), ('y', 0, 0, 0),
-    ('xr', 1, 0), ('pass', 0), ('pn', 0), ('xa', 3, 0), ('xa', 1, 0), ('y', 0, 0, 3), ('xr', 3, 0), ('y', 0, 0, 1),
-    ('near', 1), ('z', 2), ('pass', 1), ('xr', 2, 3), ('pn', 1), ('y', 0, 1, 1), ('y', 0, 1, 3), ('y', 1, 1, 0),
-    ('far', 0), ('xr', 2, 1), ('y', 1, 0, 1), ('own', 3), ('xr', 1, 1), ('xr', 1, 3), ('y', 1, 0, 3), ('xf', 0),
-    ('pf', 0), ('y', 0, 0, 2), ('y', 0, 2, 0), ('near', 2), ('pass', 2), ('y', 1, 1, 3), ('xa', 1, 1), ('xr', 2, 2),
-    ('y', 1, 1, 1), ('z', 3), ('pn', 2), ('y', 0, 2, 3), ('y', 0, 2, 1), ('far', 1), ('xr', 3, 1), ('xa', 3, 1),
-    ('y', 2, 0, 3), ('y', 1, 0, 0), ('y', 1, 0, 2), ('far', 2), ('pf', 1), ('y', 0, 1, 2), ('pf', 2), ('y', 0, 2, 2),
-    ('xr', 3, 2), ('ly', 0, 0, 0), ('y', 2, 0, 1), ('xr', 1, 2), ('y', 1, 2, 3), ('y', 0, 3, 0), ('y', 1, 2, 1),
-    ('xa', 3, 2), ('pass', 3), ('near', 3), ('y', 1, 1, 2), ('y', 1, 2, 0), ('xa', 3, 3), ('xa', 1, 2),
-    ('y', 2, 0, 0), ('y', 1, 2, 2), ('pn', 3), ('y', 0, 3, 3), ('y', 0, 3, 1), ('far', 3), ('y', 2, 1, 1),
-    ('y', 2, 1, 2), ('xa', 1, 3), ('xr', 3, 3), ('y', 2, 1, 3), ('pf', 3), ('y', 0, 3, 2), ('xf', 1), ('xf', 2),
-    ('ly', 0, 2, 0), ('y', 2, 1, 0), ('y', 2, 2, 2), ('y', 2, 0, 2), ('ly', 1, 0, 0), ('y', 2, 2, 1), ('lx', 0),
-    ('y', 1, 3, 1), ('y', 1, 3, 3), ('lx', 2), ('y', 2, 2, 0), ('y', 2, 2, 3), ('ly', 0, 1, 0), ('lx', 5), ('xf', 3),
-    ('ly', 0, 3, 0), ('y', 1, 3, 2), ('lx', 4), ('lx', 1), ('ly', 1, 3, 0), ('y', 1, 3, 0), ('ly', 2, 0, 0),
-    ('ly', 1, 2, 0), ('ly', 1, 1, 0), ('left', 0), ('y', 2, 3, 3), ('y', 2, 3, 0), ('y', 2, 3, 2), ('y', 2, 3, 1),
-    ('lx', 9), ('ly', 2, 2, 0), ('ly', 2, 1, 0), ('ly', 2, 3, 0),
+    ('own', 0), ('z', 1), ('xr', 2, 0), ('own', 1), ('own', 2), ('near', 0), ('xr', 1, 0), ('y', 0, 0, 0),
+    ('xr', 3, 0), ('pn', 0), ('pass', 0), ('z', 2), ('xr', 2, 1), ('xa', 3, 0), ('y', 0, 0, 1), ('xa', 1, 0),
+    ('y', 0, 0, 3), ('near', 1), ('y', 0, 1, 0), ('xr', 2, 3), ('pn', 1), ('y', 0, 1, 3), ('y', 0, 1, 1), ('own', 3),
+    ('pass', 1), ('far', 0), ('y', 1, 0, 1), ('y', 1, 0, 3), ('y', 1, 0, 0), ('y', 0, 2, 0), ('pf', 0), ('xr', 2, 2),
+    ('y', 0, 0, 2), ('near', 2), ('pass', 2), ('y', 0, 3, 0), ('z', 3), ('y', 1, 1, 1), ('xr', 1, 3), ('y', 1, 1, 3),
+    ('xa', 1, 3), ('pn', 2), ('far', 1), ('xr', 3, 3), ('y', 0, 2, 1), ('y', 0, 2, 3), ('xf', 0), ('pf', 1),
+    ('far', 2), ('xa', 3, 3), ('xr', 1, 2), ('y', 1, 2, 0), ('y', 1, 0, 2), ('y', 0, 1, 2), ('pf', 2), ('xr', 3, 2),
+    ('y', 1, 3, 0), ('y', 2, 0, 1), ('y', 2, 0, 3), ('y', 0, 2, 2), ('xa', 3, 2), ('y', 2, 0, 0), ('pass', 3),
+    ('near', 3), ('xa', 1, 2), ('y', 1, 1, 2), ('xa', 3, 1), ('y', 1, 2, 1), ('y', 1, 2, 3), ('xr', 3, 1),
+    ('y', 1, 1, 0), ('y', 1, 2, 2), ('pn', 3), ('y', 0, 3, 1), ('y', 2, 2, 0), ('y', 0, 3, 3), ('xr', 1, 1),
+    ('y', 2, 0, 2), ('y', 2, 1, 2), ('far', 3), ('xf', 3), ('y', 2, 2, 2), ('xa', 1, 1), ('pf', 3), ('y', 0, 3, 2),
+    ('xf', 2), ('ly', 0, 2, 0), ('y', 2, 2, 1), ('ly', 0, 0, 0), ('y', 2, 2, 3), ('ly', 0, 3, 0), ('y', 2, 1, 3),
+    ('y', 2, 3, 0), ('y', 2, 1, 0), ('lx', 0), ('xf', 1), ('ly', 0, 1, 0), ('y', 2, 1, 1), ('lx', 5), ('y', 1, 3, 1),
+    ('lx', 2), ('ly', 1, 2, 0), ('y', 1, 3, 3), ('ly', 1, 0, 0), ('y', 1, 3, 2), ('lx', 4), ('ly', 1, 3, 0),
+    ('lx', 1), ('ly', 1, 1, 0), ('left', 0), ('ly', 2, 2, 0), ('y', 2, 3, 1), ('ly', 2, 0, 0), ('y', 2, 3, 3),
+    ('y', 2, 3, 2), ('lx', 9), ('ly', 2, 3, 0), ('ly', 2, 1, 0),
 )
 
 
@@ -87,7 +87,7 @@
         columns = pl.ds(pl.multiple_of(((x + step) % 4) * 128, 128), 128)
         loads.append(pltpu.make_async_copy(q_in.at[:, columns], q.at[j, z, pl.ds(0, w_in), :], load_sem.at[2 + 2 * j]))
         loads.append(pltpu.make_async_copy(q_out.at[:, columns], q.at[j, z, pl.ds(w_in, w_out), :], load_sem.at[3 + 2 * j]))
-    for load in loads:
+    for load in loads[2:] + loads[:2]:
         load.start()
 
     pl.semaphore_wait(barrier, 7)
@@ -308,6 +308,27 @@
             @pl.loop(0, 2)
             def _(b):
                 finish(box_y, y_part(3, i, b), 25 + 3 * b, 29 - 3 * b)
+
+    query = lax.broadcasted_iota(jnp.int32, (8, 128), 0)
+    owner = lax.broadcasted_iota(jnp.int32, (8, 128), 1) // R
+
+    mask = jnp.concatenate([
+        jnp.where((owner == query + 2 * which) & (query < 2), 1.0, 0.0).astype(BF16) for which in (core, 1 - core)], axis=0)
+    rows = half // 4
+
+    def score(g):
+        line = pl.ds(g * rows, rows)
+        product = part[3, y, 0, line, :] * part[3, y, 1, line, :] * (1.0 / math.sqrt(R))
+        high = product.astype(BF16)
+        rest = product - high.astype(F32)
+        middle = rest.astype(BF16)
+        low = (rest - middle.astype(F32)).astype(BF16)
+        total = None
+        for term in (low, middle, high):
+            s = lax.dot_general(mask, term, (((1,), (1,)), ((), ())), preferred_element_type=F32)
+            total = s if total is None else total + s
+        mine[0, :, line] = total[:8]
+        theirs[0, :, line] = total[8:]
 
     def task(name, *index):
         k = index[0]
@@ -374,37 +395,17 @@
             over_y(k, i, box_x, lambda kind: 24 + 6 * c + kind, lambda b: x_part(3, i, b, c, CUTS))
         else:
             own_place(functools.partial(last_x, k))
+            if k == 9:
+                score(3)
 
     right, left = at(dx=1), at(dx=-1)
     for name, *index in TASKS:
         task(name, *index)
-
-    query = lax.broadcasted_iota(jnp.int32, (8, 128), 0)
-    owner = lax.broadcasted_iota(jnp.int32, (8, 128), 1) // R
-
-    mask = jnp.concatenate([
-        jnp.where((owner == query + 2 * which) & (query < 2), 1.0, 0.0).astype(BF16) for which in (core, 1 - core)], axis=0)
-    rows = half // 4
-    for g in range(4):
-        line = pl.ds(g * rows, rows)
-        product = part[3, y, 0, line, :] * part[3, y, 1, line, :] * (1.0 / math.sqrt(R))
-        high = product.astype(BF16)
-        rest = product - high.astype(F32)
-        middle = rest.astype(BF16)
-        low = (rest - middle.astype(F32)).astype(BF16)
-        total = None
-        for term in (low, middle, high):
-            s = lax.dot_general(mask, term, (((1,), (1,)), ((), ())), preferred_element_type=F32)
-            total = s if total is None else total + s
-        mine[0, :, line] = total[:8]
-        theirs[0, :, line] = total[8:]
+    for g in range(3):
+        score(g)
     final = copy(theirs.at[0], theirs.at[1], end_send, end_recv, at(other=True))
     final.start()
     out[:, pl.ds(pl.multiple_of(own, half), half)] = mine[0, pl.ds(0, 2), :]
-    final.wait_recv()
-    out[:, pl.ds(pl.multiple_of(partner_rows, half), half)] = theirs[1, pl.ds(0, 2), :]
-
-    final.wait_send()
     sends_left((3,))
     for i in range(4):
         for c in range(CUTS):
@@ -416,6 +417,9 @@
             left_box(box_y, 24 + kind, rows_y[i])
 
     own_place(last_left)
+    final.wait_recv()
+    out[:, pl.ds(pl.multiple_of(partner_rows, half), half)] = theirs[1, pl.ds(0, 2), :]
+    final.wait_send()
 
 
 def scores_of(act, grad, q_in, q_out):

time: 73.4 us -> 73.3 us (level); the launches traced: 72.3 us -> 73.2 us
  Pallas kernels: 71 us -> 71.8 us
    pallas_call x1, Pallas kernels: 71 us -> 71.8 us  [scores_of(): pl.pallas_call(kernel, out_shape=jax.ShapeDtypeStruct((2, tokens), F32),...]
where the time goes in v6:
time: 73.3 us; the launch traced here: 73.2 us
  Pallas kernels  71.8 us (98%)
  local copies, waits for them, and re-layouts  1.32 us (2%)
    pallas_call x1, Pallas kernels, scores_of(): pl.pallas_call(kernel, out_shape=jax.ShapeDtypeStruct((2, tokens), F32),...  71.8 us

profile of v6, /device:TPU:1, one launch (start us, length us, event | category | flops | bytes accessed | tf_op | source)
XLA Modules:
  0.0 73.2 jit_solution(1313571527034823389)
XLA Ops:
  0.0 71.8 %shard_map.46 = f32[2,2048]{1,0:T(2,128)} custom-call(bf16[2048,256]{1,0:T(8,128)(2,1)} %act.1, bf16[2048,896]{1,0:T(8,128)(2,1)} %grad.1, bf16[256,512]{1,0:T(8,128)(2,1)} %q_in.1, bf16[896,512]{1,0:T(8,128)(2,1)} %q_out.1), custom_call_target="tpu_custom_call" | custom-call | flops 9663676416 | bytes 6291456 | tf_op jit(solution)/shard_map/pallas_call | solution.py:432
  71.8 1.3 %copy.6 = f32[2048,2]{0,1:T(2,128)} copy(f32[2048,2]{0,1:T(2,128)} %bitcast.1) | data formatting | bytes 32768
